TPU v7x, 128 devices: a whole 4x4x4 slice. The times are simulated.
128 devices in a mesh: dev: 128 (over y, x, z, core).
Axes of the slice: x: 4, y: 4, z: 4, core: 2. Of those that a mesh axis runs over, the one named last changes fastest.
Arguments:
- params: float32 [59, 1048576], P(None, 'dev'), as said below
- entry_shard: int32 [2048, 128], P('dev'), may hold values from 0 to 127, as said below
- entry_row: int32 [2048, 128], P('dev'), may hold values from 0 to 8191
- depth_order: int32 [2048, 128], P('dev'), may hold values from 0 to 127, as said below
- live_count: int32 [2048], P('dev'), may hold values from 32 to 128
- tile_of_slot: int32 [2048], P('dev'), may hold values from 0 to 32399, as said below
- prev_slot: int32 [2048], P('dev'), may hold values from 0 to 2047, as said below
- gt_image: bfloat16 [2048, 768], P('dev'), may hold values from 0 to 1
Outputs:
- param_grads: float32 [59, 1048576], P(None, 'dev')
- rendered: float32 [2048, 768], P('dev')
- tile_loss: float32 [2048], P('dev')
Inputs may be any that keep to these rules, and one draw needn't show every extreme that they name: `entry_shard`: among the 2048 entries of one device's 16 slots at most 32 name any one device, and in every such block some device is named exactly 32 times. `depth_order`: each row is a permutation of 0 to 127. `tile_of_slot`: 2048 different tiles of the 240 x 135 grid, numbered row by row. `prev_slot`: A permutation of 0 to 2047; the 16 slots of one device take their previous slots from 16 different devices, one each, and each device's previous slots go to 16 different devices, one each. `params`: row 2 lies between 2 and 34 and row 6 between 0.5 and 1.5.
All inputs are finite; a program needn't handle non-finite values.
Results may differ from a plain program's by a relative error of at most 0.0003.
Values may be sent and summed in bfloat16 or wider, within the bound.
No kernel may reach another device: no remote copies, remote signals or barrier semaphores. Data moves between devices by JAX's collectives and lax.ppermute only.
A program may use at most 128 MiB of HBM per device.

v0:
```python
import jax
import jax.numpy as jnp
from jax import lax
from jax.experimental import pallas as pl
from jax.experimental.pallas import tpu as pltpu
from jax.sharding import PartitionSpec as P

TW = 240
TH = 135
FOCAL = 1200.0
LOG2E = 1.4426950408889634
F32 = jnp.float32
BF16 = jnp.bfloat16
I32 = jnp.int32


def iota(shape, axis):
    return lax.broadcasted_iota(I32, shape, axis)


def take_lane(table, index):
    return jnp.take_along_axis(table, index, axis=1, mode="promise_in_bounds")


def geometry(values):
    (pos_x, pos_y, depth, ls0, ls1, ls2, q0, q1, q2, q3, logit) = values
    scales = [jnp.exp(ls0), jnp.exp(ls1), jnp.exp(ls2)]
    inverse_q = lax.rsqrt(q0 * q0 + q1 * q1 + q2 * q2 + q3 * q3)
    w_part = q0 * inverse_q
    x_part = q1 * inverse_q
    y_part = q2 * inverse_q
    z_part = q3 * inverse_q
    rotation = [
        [
            1.0 - 2.0 * (y_part * y_part + z_part * z_part),
            2.0 * (x_part * y_part - w_part * z_part),
            2.0 * (x_part * z_part + w_part * y_part),
        ],
        [
            2.0 * (x_part * y_part + w_part * z_part),
            1.0 - 2.0 * (x_part * x_part + z_part * z_part),
            2.0 * (y_part * z_part - w_part * x_part),
        ],
        [
            2.0 * (x_part * z_part - w_part * y_part),
            2.0 * (y_part * z_part + w_part * x_part),
            1.0 - 2.0 * (x_part * x_part + y_part * y_part),
        ],
    ]
    inverse_z = 1.0 / depth
    focal_z = FOCAL * inverse_z
    ratio_x = pos_x * inverse_z
    ratio_y = pos_y * inverse_z
    slope_x = -focal_z * ratio_x
    slope_y = -focal_z * ratio_y
    first = [(focal_z * rotation[0][i] + slope_x * rotation[2][i]) * scales[i] for i in range(3)]
    second = [(focal_z * rotation[1][i] + slope_y * rotation[2][i]) * scales[i] for i in range(3)]
    spread_xx = first[0] * first[0] + first[1] * first[1] + first[2] * first[2] + 0.3
    spread_xy = first[0] * second[0] + first[1] * second[1] + first[2] * second[2]
    spread_yy = second[0] * second[0] + second[1] * second[1] + second[2] * second[2] + 0.3
    inverse_det = 1.0 / (spread_xx * spread_yy - spread_xy * spread_xy)
    inverse_norm = lax.rsqrt(pos_x * pos_x + pos_y * pos_y + depth * depth)
    return (
        FOCAL * pos_x / depth + 8.0 * TW,
        FOCAL * pos_y / depth + 8.0 * TH,
        spread_yy * inverse_det,
        -spread_xy * inverse_det,
        spread_xx * inverse_det,
        lax.logistic(logit),
        pos_x * inverse_norm,
        pos_y * inverse_norm,
        depth * inverse_norm,
    )


def harmonics(unit_x, unit_y, unit_z):
    square_x = unit_x * unit_x
    square_y = unit_y * unit_y
    square_z = unit_z * unit_z
    return [
        0.28209479177387814 * jnp.ones_like(unit_x),
        -0.4886025119029199 * unit_y,
        0.4886025119029199 * unit_z,
        -0.4886025119029199 * unit_x,
        1.0925484305920792 * unit_x * unit_y,
        -1.0925484305920792 * unit_y * unit_z,
        0.31539156525252005 * (2.0 * square_z - square_x - square_y),
        -1.0925484305920792 * unit_x * unit_z,
        0.5462742152960396 * (square_x - square_y),
        -0.5900435899266435 * unit_y * (3.0 * square_x - square_y),
        2.890611442640554 * unit_x * unit_y * unit_z,
        -0.4570457994644658 * unit_y * (4.0 * square_z - square_x - square_y),
        0.3731763325901154 * unit_z * (2.0 * square_z - 3.0 * square_x - 3.0 * square_y),
        -0.4570457994644658 * unit_x * (4.0 * square_z - square_x - square_y),
        1.445305721320277 * unit_z * (square_x - square_y),
        -0.5900435899266435 * unit_x * (square_x - 3.0 * square_y),
    ]


def route_kernel(
    shard_ref, row_ref, order_ref, live_ref, prev_ref,
    request_ref, holder_ref, place_ref, back_j_ref, back_t_ref,
):
    tiles, length = shard_ref.shape
    order = order_ref[...]
    shards = take_lane(shard_ref[...], order)
    rows = take_lane(row_ref[...], order)
    sub = iota((128, 128), 0)
    lane = iota((128, 128), 1)
    wide_row = iota((128, 256), 0)
    wide_lane = iota((128, 256), 1)
    counter = jnp.where((wide_lane >= 128) | (wide_row < wide_lane), 1.0, 0.0).astype(BF16)
    sub_k = iota((32, 128), 0)
    j_code = iota((1, 128), 1).astype(F32)
    carry = jnp.zeros((128, 128), F32)
    request = jnp.zeros((128, 128), F32)
    back = jnp.zeros((64, 128), F32)
    truth = jnp.zeros((128, 128), I32)
    nothing = jnp.zeros((96, 256), F32)
    for t in range(tiles):
        live = order[t : t + 1, :] < live_ref[t]
        holder = jnp.where(live, shards[t : t + 1, :], -1)
        match = jnp.broadcast_to(holder, (128, 128)) == sub
        hot = jnp.where(match, 1.0, 0.0).astype(BF16)
        counted = jnp.dot(hot, counter, preferred_element_type=F32)
        place = jnp.sum(
            jnp.where(match, counted[:, :128] + carry, 0.0), axis=0, keepdims=True
        ).astype(I32)
        carry = carry + counted[:, 128:]
        holder_ref[t : t + 1, :] = holder
        place_ref[t : t + 1, :] = jnp.where(live, place, -1)
        match_k = jnp.broadcast_to(place, (32, 128)) == sub_k
        row = rows[t : t + 1, :]
        high = jnp.where(match_k, ((row >> 7) * 128).astype(F32), 0.0)
        low = jnp.where(match_k, (row & 127).astype(F32), 0.0)
        asked = jnp.concatenate(
            [jnp.concatenate([high, low], axis=1), nothing], axis=0
        ).astype(BF16)
        request = request + lax.dot_general(
            jnp.concatenate([hot, hot], axis=1), asked,
            (((1,), (1,)), ((), ())), preferred_element_type=F32,
        )
        codes = jnp.concatenate(
            [jnp.where(match_k, j_code, 0.0), jnp.where(match_k, t + 1.0, 0.0)], axis=0
        ).astype(BF16)
        back = back + lax.dot_general(
            codes, hot, (((1,), (1,)), ((), ())), preferred_element_type=F32
        )
        previous = prev_ref[t]
        truth = jnp.where(sub == lax.shift_right_logical(previous, 4), previous & 15, truth)
    request_ref[...] = jnp.where(lane == 32, truth, request.astype(I32))
    back_j_ref[...] = back[:32, :].astype(I32)
    back_t_ref[...] = back[32:, :].astype(I32) - 1


def project_kernel(params_ref, out_ref):
    def step(block, unused):
        start = pl.multiple_of(block * 1024, 1024)
        values = params_ref[:, pl.ds(start, 1024)].reshape(59, 8, 128)
        p = [values[i] for i in range(59)]
        (u, v, ca, cb, cc, opacity, ux, uy, uz) = geometry(p[:11])
        basis = harmonics(ux, uy, uz)
        colors = []
        for channel in range(3):
            color = 0.5 + basis[0] * p[11 + 16 * channel]
            for degree in range(1, 16):
                color = color + basis[degree] * p[11 + 16 * channel + degree]
            colors.append(color)
        for c, value in enumerate([u, v, ca, cb, cc] + colors + [opacity]):
            out_ref[c, pl.ds(pl.multiple_of(block * 8, 8), 8), :] = value
        return unused

    lax.fori_loop(0, 8, step, 0)


def pick_kernel(asked_ref, table_ref, out_ref):
    index = asked_ref[...].astype(F32).T[:32, :].astype(I32)
    high = index >> 7
    low = index & 127
    zeros = tuple(jnp.zeros((32, 128), F32) for _ in range(9))

    def step(h, sums):
        match = high == h
        return tuple(
            jnp.where(
                match,
                take_lane(jnp.broadcast_to(table_ref[c, pl.ds(h, 1), :], (32, 128)), low),
                sums[c],
            )
            for c in range(9)
        )

    found = lax.fori_loop(0, 64, step, zeros, unroll=4)
    put_rows(out_ref, found)


def put_rows(out_ref, found):
    blank = jnp.zeros((96, 128), F32)
    for i in range(3):
        group = list(found[4 * i : 4 * i + 4])
        if i == 2:
            group.append(blank)
        out_ref[pl.ds(i, 128, stride=3), :] = jnp.concatenate(group, axis=0).T


def truth_kernel(asked_ref, image_ref, out_ref):
    hot = jnp.where(asked_ref[:, 32:33] == iota((128, 16), 1), 1.0, 0.0).astype(BF16)
    out_ref[...] = jnp.dot(hot, image_ref[...], preferred_element_type=F32).astype(BF16)


def render_kernel(
    arrived_ref, holder_ref, place_ref, back_j_ref, back_t_ref, delivered_ref, tile_ref, prev_ref,
    picture_ref, loss_ref, out_ref,
    table_ref, ordered_ref, alpha_ref, weight_ref, reach_ref, grad_ref,
):
    for i in range(3):
        table_ref[128 * i : 128 * (i + 1), :] = arrived_ref[pl.ds(i, 128, stride=3), :].T
    holder = jnp.maximum(holder_ref[...], 0)
    place = place_ref[...]
    values = [jnp.zeros((16, 128), F32) for _ in range(9)]
    for k in range(32):
        match = place == k
        for c in range(9):
            row = jnp.broadcast_to(table_ref[32 * c + k : 32 * c + k + 1, :], (16, 128))
            values[c] = jnp.where(match, take_lane(row, holder), values[c])
    sub = iota((16, 128), 0)
    base_x = jnp.zeros((16, 128), F32)
    base_y = jnp.zeros((16, 128), F32)
    source = jnp.zeros((16, 128), I32)
    for t in range(16):
        number = tile_ref[t]
        tile_row = number // TW
        tile_column = number - tile_row * TW
        base_x = jnp.where(sub == t, (16 * tile_column + 8).astype(F32), base_x)
        base_y = jnp.where(sub == t, (16 * tile_row + 8).astype(F32), base_y)
        source = jnp.where(sub == t, lax.shift_right_logical(prev_ref[t], 4), source)
    (u, v, ca, cb, cc, red, green, blue, opacity) = values
    u = u - base_x
    v = v - base_y
    for c, value in enumerate(
        [u, v, (-0.5 * LOG2E) * ca, (-LOG2E) * cb, (-0.5 * LOG2E) * cc, red, green, blue, opacity]
    ):
        ordered_ref[c] = value
    pixel = iota((8, 128), 1)
    grid_x = (pixel & 15).astype(F32) - 7.5
    grid_y = [(pixel >> 4).astype(F32) - 7.5, (pixel >> 4).astype(F32) + 0.5]

    def column(c, g, j):
        return take_lane(
            ordered_ref[c, 8 * g : 8 * g + 8, :], jnp.full((8, 128), j, I32)
        )

    ones = jnp.ones((8, 128), F32)
    zero = jnp.zeros((8, 128), F32)

    def forward(j, state):
        reach, sums = state
        reach = list(reach)
        sums = list(sums)
        for g in range(2):
            (gu, gv, ga, gb, gc, g0, g1, g2, go) = [column(c, g, j) for c in range(9)]
            dx = grid_x - gu
            part_a = ga * dx * dx
            part_b = gb * dx
            for h in range(2):
                n = 2 * g + h
                dy = grid_y[h] - gv
                fall = jnp.exp2(part_a + dy * (part_b + gc * dy))
                alpha = go * fall
                weight = alpha * reach[n]
                alpha_ref[j, n] = alpha
                weight_ref[j, n] = weight
                reach_ref[j, n] = fall * reach[n]
                reach[n] = reach[n] - weight
                sums[3 * n] = sums[3 * n] + weight * g0
                sums[3 * n + 1] = sums[3 * n + 1] + weight * g1
                sums[3 * n + 2] = sums[3 * n + 2] + weight * g2
        return (tuple(reach), tuple(sums))

    unused, sums = lax.fori_loop(
        0, 128, forward, (tuple([ones] * 4), tuple([zero] * 12)), unroll=4
    )
    hot = jnp.where(source == iota((16, 128), 1), 1.0, 0.0).astype(BF16)
    target = jnp.dot(hot, delivered_ref[...], preferred_element_type=F32)
    loss = jnp.zeros((16, 1), F32)
    slopes = []
    for k in range(3):
        image = jnp.concatenate(
            [
                jnp.concatenate([sums[3 * (2 * g) + k], sums[3 * (2 * g + 1) + k]], axis=1)
                for g in range(2)
            ],
            axis=0,
        )
        picture_ref[:, 256 * k : 256 * (k + 1)] = image
        wanted = target[:, 256 * k : 256 * (k + 1)]
        difference = image - wanted
        smooth = jnp.sqrt(difference * difference + 0.0001)
        mean_r = jnp.sum(image, axis=1, keepdims=True) / 256.0
        mean_t = jnp.sum(wanted, axis=1, keepdims=True) / 256.0
        centered_r = image - mean_r
        centered_t = wanted - mean_t
        var_r = jnp.sum(centered_r * centered_r, axis=1, keepdims=True) / 256.0
        var_t = jnp.sum(centered_t * centered_t, axis=1, keepdims=True) / 256.0
        cov = jnp.sum(centered_r * centered_t, axis=1, keepdims=True) / 256.0
        top_m = 2.0 * mean_r * mean_t + 0.0001
        top_c = 2.0 * cov + 0.0009
        low_m = mean_r * mean_r + mean_t * mean_t + 0.0001
        low_v = var_r + var_t + 0.0009
        below = 1.0 / (low_m * low_v)
        similarity = top_m * top_c * below
        loss = loss + (0.8 / 3.0) * jnp.sum(smooth, axis=1, keepdims=True)
        loss = loss + (0.2 * 256.0 / 3.0) * (1.0 - similarity)
        by_mean = 2.0 * mean_t * top_c * below - similarity * 2.0 * mean_r / low_m
        by_cov = 2.0 * top_m * below
        by_var = -similarity / low_v
        slopes.append(
            (0.8 / 3.0) * difference / smooth
            - (0.2 / 3.0) * (by_mean + 2.0 * by_var * centered_r + by_cov * centered_t)
        )
    loss_ref[...] = jnp.broadcast_to(loss, (16, 128))
    slope = [
        [slopes[k][8 * g : 8 * g + 8, 128 * h : 128 * h + 128] for k in range(3)]
        for g in range(2)
        for h in range(2)
    ]
    grid_yy = [grid_y[h] * grid_y[h] for h in range(2)]
    for c in range(9):
        grad_ref[c] = jnp.zeros((16, 128), F32)

    def backward(step, state):
        j = 127 - step
        behind = list(state)
        here = iota((8, 128), 1) == j
        for g in range(2):
            (g0, g1, g2) = [column(c, g, j) for c in (5, 6, 7)]
            pulls = []
            shares = []
            for h in range(2):
                n = 2 * g + h
                value = slope[n][0] * g0 + slope[n][1] * g1 + slope[n][2] * g2
                gap = value - behind[n]
                pulls.append(reach_ref[j, n] * gap)
                behind[n] = behind[n] + alpha_ref[j, n] * gap
                weight = weight_ref[j, n]
                shares.append([weight * slope[n][k] for k in range(3)])
            both = pulls[0] + pulls[1]
            tall = pulls[0] * grid_y[0] + pulls[1] * grid_y[1]
            taller = pulls[0] * grid_yy[0] + pulls[1] * grid_yy[1]
            both_x = both * grid_x
            moments = [
                both,
                both_x,
                tall,
                both_x * grid_x,
                tall * grid_x,
                taller,
                shares[0][0] + shares[1][0],
                shares[0][1] + shares[1][1],
                shares[0][2] + shares[1][2],
            ]
            for c, moment in enumerate(moments):
                total = jnp.sum(moment, axis=1, keepdims=True)
                spot = grad_ref[c, 8 * g : 8 * g + 8, :]
                grad_ref[c, 8 * g : 8 * g + 8, :] = jnp.where(here, total, spot)
        return tuple(behind)

    lax.fori_loop(0, 128, backward, tuple([zero] * 4), unroll=4)
    (m0, mx, my, mxx, mxy, myy, d_red, d_green, d_blue) = [grad_ref[c] for c in range(9)]
    sx = mx - u * m0
    sy = my - v * m0
    sxx = mxx - u * (mx + sx)
    syy = myy - v * (my + sy)
    sxy = mxy - u * my - v * sx
    results = [
        opacity * (ca * sx + cb * sy),
        opacity * (cb * sx + cc * sy),
        -0.5 * opacity * sxx,
        -opacity * sxy,
        -0.5 * opacity * syy,
        d_red,
        d_green,
        d_blue,
        m0,
    ]
    back_j = back_j_ref[...]
    back_t = back_t_ref[...]
    for c in range(9):
        grad_ref[c] = results[c]
    found = [jnp.zeros((32, 128), F32) for _ in range(9)]
    for t in range(16):
        match = back_t == t
        for c in range(9):
            row = jnp.broadcast_to(grad_ref[c, t : t + 1, :], (32, 128))
            found[c] = jnp.where(match, take_lane(row, back_j), found[c])
    put_rows(out_ref, found)


def update_kernel(returned_ref, asked_ref, params_ref, out_ref, high_ref, low_ref, piece_ref, sum_ref):
    index = asked_ref[...].astype(F32).T[:32, :].astype(I32)
    high_ref[...] = (index >> 7) & 31
    low_ref[...] = (index & 127) + 128 * (index >> 12)
    for i in range(3):
        block = returned_ref[pl.ds(i, 128, stride=3), :].T
        rows = 128 if i < 2 else 32
        block = block[:rows, :]
        upper = block.astype(BF16).astype(F32)
        piece_ref[0, 128 * i : 128 * i + rows, :] = upper
        piece_ref[1, 128 * i : 128 * i + rows, :] = block - upper
    sum_ref[...] = jnp.zeros((288, 256), F32)
    sub_high = iota((32, 128), 0)
    sub_low = iota((256, 128), 0)

    def scatter(pair, unused):
        right = []
        left = [[], []]
        for half in range(2):
            k = 2 * pair + half
            low = jnp.broadcast_to(low_ref[pl.ds(k, 1), :], (256, 128))
            right.append(jnp.where(low == sub_low, 1.0, 0.0).astype(BF16))
            high = jnp.broadcast_to(high_ref[pl.ds(k, 1), :], (32, 128)) == sub_high
            for p in range(2):
                left[p].append(
                    jnp.concatenate(
                        [
                            jnp.where(high, piece_ref[p, pl.ds(32 * c + k, 1), :], 0.0)
                            for c in range(9)
                        ],
                        axis=0,
                    ).astype(BF16)
                )
        right = jnp.concatenate(right, axis=1)
        total = sum_ref[...]
        for p in range(2):
            total = total + lax.dot_general(
                jnp.concatenate(left[p], axis=1), right,
                (((1,), (1,)), ((), ())), preferred_element_type=F32,
            )
        sum_ref[...] = total
        return unused

    lax.fori_loop(0, 16, scatter, 0)

    def pull(block, half):
        start = pl.multiple_of(half * 4096 + block * 1024, 1024)
        values = params_ref[:, pl.ds(start, 1024)].reshape(59, 8, 128)
        p = [values[i] for i in range(59)]
        g = [
            sum_ref[pl.ds(pl.multiple_of(32 * c + 8 * block, 8), 8), 128 * half : 128 * half + 128]
            for c in range(9)
        ]
        primal, pull_geometry = jax.vjp(lambda *a: geometry(a), *p[:11])
        basis, pull_basis = jax.vjp(lambda *a: tuple(harmonics(*a)), *primal[6:9])
        d_basis = tuple(
            g[5] * p[11 + i] + g[6] * p[27 + i] + g[7] * p[43 + i] for i in range(16)
        )
        d_unit = pull_basis(d_basis)
        d_first = pull_geometry((g[0], g[1], g[2], g[3], g[4], g[8]) + tuple(d_unit))
        rows = list(d_first) + [g[5 + k] * basis[i] for k in range(3) for i in range(16)]
        out_ref[:, pl.ds(start, 1024)] = jnp.stack(rows, axis=0).reshape(59, 1024)

    for half in range(2):
        lax.fori_loop(0, 4, lambda b, unused, half=half: (pull(b, half), unused)[1], 0)


def vmem():
    return pl.BlockSpec(memory_space=pltpu.VMEM)


def smem():
    return pl.BlockSpec(memory_space=pltpu.SMEM)


def shape(dims, dtype=F32):
    return jax.ShapeDtypeStruct(dims, dtype)


ROOM = pltpu.CompilerParams(vmem_limit_bytes=40 * 1024 * 1024)


def swap(values):
    return lax.all_to_all(values, "dev", split_axis=0, concat_axis=0, tiled=True)


def body(
    params, entry_shard, entry_row, depth_order, live_count, tile_of_slot, prev_slot, gt_image
):
    request, holder, place, back_j, back_t = pl.pallas_call(
        route_kernel,
        out_shape=(
            shape((128, 128), I32),
            shape((16, 128), I32),
            shape((16, 128), I32),
            shape((32, 128), I32),
            shape((32, 128), I32),
        ),
        in_specs=[vmem(), vmem(), vmem(), smem(), smem()],
        out_specs=(vmem(),) * 5,
        compiler_params=ROOM,
        name="route",
    )(entry_shard, entry_row, depth_order, live_count, prev_slot)
    asked = swap(request)
    table = pl.pallas_call(
        project_kernel,
        out_shape=shape((9, 64, 128)),
        in_specs=[vmem()],
        out_specs=vmem(),
        compiler_params=ROOM,
        name="project",
    )(params)
    picked = pl.pallas_call(
        pick_kernel,
        out_shape=shape((384, 128)),
        in_specs=[vmem(), vmem()],
        out_specs=vmem(),
        compiler_params=ROOM,
        name="pick",
    )(asked, table)
    arrived = swap(picked)
    sent_truth = pl.pallas_call(
        truth_kernel,
        out_shape=shape((128, 768), BF16),
        in_specs=[vmem(), vmem()],
        out_specs=vmem(),
        compiler_params=ROOM,
        name="truth",
    )(asked, gt_image)
    delivered = swap(sent_truth)
    picture, loss, outgoing = pl.pallas_call(
        render_kernel,
        out_shape=(shape((16, 768)), shape((16, 128)), shape((384, 128))),
        in_specs=[vmem()] * 6 + [smem(), smem()],
        out_specs=(vmem(),) * 3,
        scratch_shapes=[
            pltpu.VMEM((384, 128), F32),
            pltpu.VMEM((9, 16, 128), F32),
            pltpu.VMEM((128, 4, 8, 128), F32),
            pltpu.VMEM((128, 4, 8, 128), F32),
            pltpu.VMEM((128, 4, 8, 128), F32),
            pltpu.VMEM((9, 16, 128), F32),
        ],
        compiler_params=ROOM,
        name="render",
    )(arrived, holder, place, back_j, back_t, delivered, tile_of_slot, prev_slot)
    returned = swap(outgoing)
    gradients = pl.pallas_call(
        update_kernel,
        out_shape=shape((59, 8192)),
        in_specs=[vmem()] * 3,
        out_specs=vmem(),
        scratch_shapes=[
            pltpu.VMEM((32, 128), I32),
            pltpu.VMEM((32, 128), I32),
            pltpu.VMEM((2, 288, 128), F32),
            pltpu.VMEM((288, 256), F32),
        ],
        compiler_params=ROOM,
        name="update",
    )(returned, asked, params)
    return (gradients, picture, loss[:, 0])


def solution(mesh):
    return jax.shard_map(
        body,
        mesh=mesh,
        in_specs=(
            P(None, "dev"),
            P("dev", None),
            P("dev", None),
            P("dev", None),
            P("dev"),
            P("dev"),
            P("dev"),
            P("dev", None),
        ),
        out_specs=(P(None, "dev"), P("dev", None), P("dev")),
        check_vma=False,
    )
```

profile of v0, /device:TPU:1, one launch (start us, length us, event | category | flops | bytes accessed | tf_op | source)
XLA Modules:
  0.0 120.3 jit_solution(16468477046729855013)
XLA Ops:
  0.6 0.7 copy-done.3
  1.3 0.7 copy-done.4
  2.0 0.7 copy-done.5
  2.7 0.7 copy-done.6
  3.4 0.7 copy-done.9
  4.0 3.7 %route.1 = (s32[128,128]{1,0:T(8,128)S(1)}, s32[16,128]{1,0:T(8,128)S(1)}, s32[16,128]{1,0:T(8,128)S(1)}, s32[32,128]{1,0:T(8,128)S(1)}, s32[32,128]{1,0:T(8,128)S(1)}) custom-call(s32[16,128]{1,0:T(8,128)S(1)} %copy-done.3, s32[16,128]{1,0:T(8,128)S(1)} %copy-done.4, s32[16,128]{1,0:T(8,128)S(1)} %copy-done.5, s32[16]{0:T(128)S(1)} %copy-done.9, ...), custom_call_target="tpu_custom_call" | custom-call | tf_op jit(solution)/shard_map/route/pallas_call | solution.py:488
  7.7 20.7 %all_to_all.44 = s32[128,1,128]{2,1,0:T(1,128)S(1)} all-to-all(s32[128,1,128]{2,1,0:T(1,128)S(1)} %bitcast.13), channel_id=1, replica_groups=mesh['dev'=128] {'dev'}, dimensions={0} | all-to-all | bytes 131072 | tf_op jit(solution)/shard_map/all_to_all | solution.py:482
  28.4 0.7 copy-done.2
  29.2 0.2 truth.1
  29.4 0.5 broadcast.1
  29.9 0.7 reduce.2
  30.7 0.7 reshape.15
  31.4 4.6 %all-to-all-start.2 = ((bf16[128,2,384]{2,1,0:T(2,128)(2,1)}), bf16[128,2,384]{2,1,0:T(2,128)(2,1)S(1)}, u32[]{:S(2)}, u32[]{:S(2)}) async-start(bf16[128,2,384]{2,1,0:T(2,128)(2,1)} %reshape.15), calls=%async_computation.2 | async-start | bytes 393216 | tf_op jit(solution)/shard_map/all_to_all | solution.py:482
  36.0 0.0 copy-start
  36.0 1.6 %copy-done = f32[59,8192]{1,0:T(8,128)S(1)} copy-done((f32[59,8192]{1,0:T(8,128)S(1)}, f32[59,8192]{1,0:T(8,128)}, u32[]{:S(2)}) %copy-start) | copy-done | bytes 1933336
  37.6 0.6 project.1.table_ref
  38.2 0.0 copy-start.7
  38.3 0.0 copy-start.8
  38.3 7.8 %pick.1 = f32[384,128]{1,0:T(8,128)S(1)} custom-call(s32[128,128]{1,0:T(8,128)S(1)} %bitcast.9, f32[9,64,128]{2,1,0:T(8,128)S(1)} %project.1.table_ref), custom_call_target="tpu_custom_call" | custom-call | tf_op jit(solution)/shard_map/pick/pallas_call | solution.py:511
  46.0 0.8 all_to_all.31
  46.8 0.0 all-to-all-done.2
  46.8 9.8 %all-to-all-start.1 = ((f32[128,3,128]{2,1,0:T(4,128)}), f32[128,3,128]{2,1,0:T(4,128)S(1)}, u32[]{:S(2)}, u32[]{:S(2)}) async-start(f32[128,3,128]{2,1,0:T(4,128)} %all_to_all.31), calls=%async_computation.1 | async-start | bytes 524288 | tf_op jit(solution)/shard_map/all_to_all | solution.py:482
  56.7 0.1 reshape.16
  56.9 10.7 %all-to-all-done.1 = f32[128,3,128]{2,1,0:T(4,128)S(1)} async-done(((f32[128,3,128]{2,1,0:T(4,128)}), f32[128,3,128]{2,1,0:T(4,128)S(1)}, u32[]{:S(2)}, u32[]{:S(2)}) %all-to-all-start.1) | async-done | bytes 196640 | tf_op jit(solution)/shard_map/all_to_all | solution.py:482
  67.6 0.1 all_to_all.33.arrived_ref
  67.7 28.9 %render.1 = (f32[16,768]{1,0:T(8,128)}, f32[16,128]{1,0:T(8,128)S(1)}, f32[384,128]{1,0:T(8,128)S(1)}) custom-call(f32[384,128]{1,0:T(8,128)S(1)} %all_to_all.33.arrived_ref, s32[16,128]{1,0:T(8,128)S(1)} %get-tuple-element.12.holder_ref, s32[16,128]{1,0:T(8,128)S(1)} %get-tuple-element.13.place_ref, s32[32,128]{1,0:T(8,128)S(1)} %get-tuple-element.14.back_j_ref, ...), custom_call_target="tpu_custom_call" | custom-call | tf_op jit(solution)/shard_map/render/pallas_call | solution.py:529
  96.6 0.8 all_to_all.37
  97.4 4.5 %all-to-all-start.3 = ((f32[128,3,128]{2,1,0:T(4,128)}), f32[128,3,128]{2,1,0:T(4,128)S(1)}, u32[]{:S(2)}, u32[]{:S(2)}) async-start(f32[128,3,128]{2,1,0:T(4,128)} %all_to_all.37), calls=%async_computation.3 | async-start | bytes 524288 | tf_op jit(solution)/shard_map/all_to_all | solution.py:482
  102.0 0.6 slice_reduce_fusion
  102.6 10.4 %all-to-all-done.3 = f32[128,3,128]{2,1,0:T(4,128)S(1)} async-done(((f32[128,3,128]{2,1,0:T(4,128)}), f32[128,3,128]{2,1,0:T(4,128)S(1)}, u32[]{:S(2)}, u32[]{:S(2)}) %all-to-all-start.3) | async-done | bytes 196640 | tf_op jit(solution)/shard_map/all_to_all | solution.py:482
  113.0 0.1 all_to_all.39.returned_ref
  113.1 7.3 %update.1 = f32[59,8192]{1,0:T(8,128)} custom-call(f32[384,128]{1,0:T(8,128)S(1)} %all_to_all.39.returned_ref, s32[128,128]{1,0:T(8,128)S(1)} %bitcast.10, f32[59,8192]{1,0:T(8,128)S(1)} %copy-done.1), custom_call_target="tpu_custom_call" | custom-call | tf_op jit(solution)/shard_map/update/pallas_call | solution.py:546
  (11 shorter events, 0.0 us)
Async XLA Ops:
  0.6 0.7 copy-start.3
  1.3 0.7 copy-start.4
  2.0 0.7 copy-start.5
  2.7 0.7 copy-start.6
  3.4 0.7 copy-start.9
  28.4 0.7 copy-start.2
  31.4 15.4 %all-to-all-start.2 = ((bf16[128,2,384]{2,1,0:T(2,128)(2,1)}), bf16[128,2,384]{2,1,0:T(2,128)(2,1)S(1)}, u32[]{:S(2)}, u32[]{:S(2)}) async-start(bf16[128,2,384]{2,1,0:T(2,128)(2,1)} %reshape.15), calls=%async_computation.2 | async-start | bytes 393216 | tf_op jit(solution)/shard_map/all_to_all | solution.py:482
  36.0 1.6 %copy-start = (f32[59,8192]{1,0:T(8,128)S(1)}, f32[59,8192]{1,0:T(8,128)}, u32[]{:S(2)}) copy-start(f32[59,8192]{1,0:T(8,128)} %params_ref.3) | copy-start | bytes 5799940
  38.2 29.4 %copy-start.7 = (s32[16]{0:T(128)S(1)}, s32[16]{0:T(128)}, u32[]{:S(2)}) copy-start(s32[16]{0:T(128)} %prev_ref.3) | copy-start | bytes 196
  38.3 29.4 %copy-start.8 = (s32[16]{0:T(128)S(1)}, s32[16]{0:T(128)}, u32[]{:S(2)}) copy-start(s32[16]{0:T(128)} %tile_ref.1) | copy-start | bytes 196
  46.8 66.2 %copy-start.1 = (f32[59,8192]{1,0:T(8,128)S(1)}, f32[59,8192]{1,0:T(8,128)}, u32[]{:S(2)}) copy-start(f32[59,8192]{1,0:T(8,128)} %params_ref.3) | copy-start | bytes 5799940
  46.8 20.7 %all-to-all-start.1 = ((f32[128,3,128]{2,1,0:T(4,128)}), f32[128,3,128]{2,1,0:T(4,128)S(1)}, u32[]{:S(2)}, u32[]{:S(2)}) async-start(f32[128,3,128]{2,1,0:T(4,128)} %all_to_all.31), calls=%async_computation.1 | async-start | bytes 524288 | tf_op jit(solution)/shard_map/all_to_all | solution.py:482
  97.4 15.6 %all-to-all-start.3 = ((f32[128,3,128]{2,1,0:T(4,128)}), f32[128,3,128]{2,1,0:T(4,128)S(1)}, u32[]{:S(2)}, u32[]{:S(2)}) async-start(f32[128,3,128]{2,1,0:T(4,128)} %all_to_all.37), calls=%async_computation.3 | async-start | bytes 524288 | tf_op jit(solution)/shard_map/all_to_all | solution.py:482
where the time goes:
time: 121 us; the launch traced here: 120 us
  Pallas kernels  48.5 us (40%)
  waiting for transfers between devices  21.1 us (17%)
  blocking collectives  20.7 us (17%)
  starting transfers between devices  19 us (16%)
  local copies, waits for them, and re-layouts  9.53 us (8%)
    pallas_call x1, Pallas kernels, body(): pl.pallas_call(render_kernel, out_shape=(shape((16, 768)), shape((16, 128...  28.9 us
    all_to_all x3, waiting for transfers between devices, swap(): lax.all_to_all(values, 'dev', split_axis=0, concat_axis=0, tiled=True)  21.1 us
    all_to_all x1, blocking collectives, swap(): lax.all_to_all(values, 'dev', split_axis=0, concat_axis=0, tiled=True)  20.7 us
    all_to_all x3, starting transfers between devices, swap(): lax.all_to_all(values, 'dev', split_axis=0, concat_axis=0, tiled=True)  19 us
    pallas_call x1, Pallas kernels, body(): pl.pallas_call(pick_kernel, out_shape=shape((384, 128)), in_specs=[vmem()...  7.77 us
    pallas_call x1, Pallas kernels, body(): pl.pallas_call(update_kernel, out_shape=shape((59, 8192)), in_specs=[vmem...  7.26 us
    unnamed x23, local copies, waits for them, and re-layouts  6.63 us
    pallas_call x1, Pallas kernels, body(): pl.pallas_call(route_kernel, out_shape=(shape((128, 128), I32), shape((16...  3.68 us
  transfers between devices with their start and end apart: 3, of which 2 were waited for; matrix products, arithmetic and copies ran while one was open for 1% of the time, Pallas kernels for 7%

commit v1 on v0

v1 whole, which is shorter than its diff:
```python
import jax
import jax.numpy as jnp
from jax import lax
from jax.experimental import pallas as pl
from jax.experimental.pallas import tpu as pltpu
from jax.sharding import PartitionSpec as P

TW = 240
TH = 135
FOCAL = 1200.0
LOG2E = 1.4426950408889634
F32 = jnp.float32
BF16 = jnp.bfloat16
I32 = jnp.int32


def iota(shape, axis):
    return lax.broadcasted_iota(I32, shape, axis)


def take_lane(table, index):
    return jnp.take_along_axis(table, index, axis=1, mode="promise_in_bounds")


def geometry(values):
    (pos_x, pos_y, depth, ls0, ls1, ls2, q0, q1, q2, q3, logit) = values
    scales = [jnp.exp(ls0), jnp.exp(ls1), jnp.exp(ls2)]
    inverse_q = lax.rsqrt(q0 * q0 + q1 * q1 + q2 * q2 + q3 * q3)
    w_part = q0 * inverse_q
    x_part = q1 * inverse_q
    y_part = q2 * inverse_q
    z_part = q3 * inverse_q
    rotation = [
        [
            1.0 - 2.0 * (y_part * y_part + z_part * z_part),
            2.0 * (x_part * y_part - w_part * z_part),
            2.0 * (x_part * z_part + w_part * y_part),
        ],
        [
            2.0 * (x_part * y_part + w_part * z_part),
            1.0 - 2.0 * (x_part * x_part + z_part * z_part),
            2.0 * (y_part * z_part - w_part * x_part),
        ],
        [
            2.0 * (x_part * z_part - w_part * y_part),
            2.0 * (y_part * z_part + w_part * x_part),
            1.0 - 2.0 * (x_part * x_part + y_part * y_part),
        ],
    ]
    inverse_z = 1.0 / depth
    focal_z = FOCAL * inverse_z
    ratio_x = pos_x * inverse_z
    ratio_y = pos_y * inverse_z
    slope_x = -focal_z * ratio_x
    slope_y = -focal_z * ratio_y
    first = [(focal_z * rotation[0][i] + slope_x * rotation[2][i]) * scales[i] for i in range(3)]
    second = [(focal_z * rotation[1][i] + slope_y * rotation[2][i]) * scales[i] for i in range(3)]
    spread_xx = first[0] * first[0] + first[1] * first[1] + first[2] * first[2] + 0.3
    spread_xy = first[0] * second[0] + first[1] * second[1] + first[2] * second[2]
    spread_yy = second[0] * second[0] + second[1] * second[1] + second[2] * second[2] + 0.3
    inverse_det = 1.0 / (spread_xx * spread_yy - spread_xy * spread_xy)
    inverse_norm = lax.rsqrt(pos_x * pos_x + pos_y * pos_y + depth * depth)
    return (
        FOCAL * pos_x / depth + 8.0 * TW,
        FOCAL * pos_y / depth + 8.0 * TH,
        spread_yy * inverse_det,
        -spread_xy * inverse_det,
        spread_xx * inverse_det,
        lax.logistic(logit),
        pos_x * inverse_norm,
        pos_y * inverse_norm,
        depth * inverse_norm,
    )


def harmonics(unit_x, unit_y, unit_z):
    square_x = unit_x * unit_x
    square_y = unit_y * unit_y
    square_z = unit_z * unit_z
    return [
        0.28209479177387814 * jnp.ones_like(unit_x),
        -0.4886025119029199 * unit_y,
        0.4886025119029199 * unit_z,
        -0.4886025119029199 * unit_x,
        1.0925484305920792 * unit_x * unit_y,
        -1.0925484305920792 * unit_y * unit_z,
        0.31539156525252005 * (2.0 * square_z - square_x - square_y),
        -1.0925484305920792 * unit_x * unit_z,
        0.5462742152960396 * (square_x - square_y),
        -0.5900435899266435 * unit_y * (3.0 * square_x - square_y),
        2.890611442640554 * unit_x * unit_y * unit_z,
        -0.4570457994644658 * unit_y * (4.0 * square_z - square_x - square_y),
        0.3731763325901154 * unit_z * (2.0 * square_z - 3.0 * square_x - 3.0 * square_y),
        -0.4570457994644658 * unit_x * (4.0 * square_z - square_x - square_y),
        1.445305721320277 * unit_z * (square_x - square_y),
        -0.5900435899266435 * unit_x * (square_x - 3.0 * square_y),
    ]


def split(value, pieces):
    parts = []
    for _ in range(pieces - 1):
        part = value.astype(BF16)
        parts.append(part)
        value = value - part.astype(F32)
    parts.append(value.astype(BF16))
    return parts


def contract_lanes(left, right):
    return lax.dot_general(left, right, (((1,), (1,)), ((), ())), preferred_element_type=F32)


def indicator(condition):
    return jnp.where(condition, 1.0, 0.0).astype(BF16)


def spread(row, count):
    return jnp.broadcast_to(row, (count, row.shape[1]))


def route_kernel(
    shard_hbm, row_hbm, order_hbm, live_hbm, prev_hbm, request_ref, holder_ref, place_ref,
    shard_ref, row_ref, order_ref, live_ref, prev_ref, sems,
):
    tiles, length = shard_ref.shape
    copies = [
        pltpu.make_async_copy(source, target, sems.at[n])
        for n, (source, target) in enumerate(
            [
                (order_hbm, order_ref),
                (shard_hbm, shard_ref),
                (row_hbm, row_ref),
                (live_hbm, live_ref),
                (prev_hbm, prev_ref),
            ]
        )
    ]
    for copy in copies:
        copy.start()
    for copy in copies:
        copy.wait()
    order = order_ref[...]
    shards = take_lane(shard_ref[...], order)
    rows = take_lane(row_ref[...], order)
    sub = iota((128, 128), 0)
    lane = iota((128, 128), 1)
    wide_row = iota((128, 256), 0)
    wide_lane = iota((128, 256), 1)
    counter = indicator((wide_lane >= 128) | (wide_row < wide_lane))
    sub_k = iota((32, 128), 0)
    carry = jnp.zeros((128, 128), F32)
    request = jnp.zeros((128, 128), F32)
    truth = jnp.zeros((128, 128), I32)
    nothing = jnp.zeros((96, 256), F32)
    for t in range(tiles):
        live = order[t : t + 1, :] < live_ref[t]
        holder = jnp.where(live, shards[t : t + 1, :], -1)
        match = spread(holder, 128) == sub
        hot = indicator(match)
        counted = jnp.dot(hot, counter, preferred_element_type=F32)
        place = jnp.sum(
            jnp.where(match, counted[:, :128] + carry, 0.0), axis=0, keepdims=True
        ).astype(I32)
        carry = carry + counted[:, 128:]
        holder_ref[t : t + 1, :] = holder
        place_ref[t : t + 1, :] = jnp.where(live, place, -1)
        match_k = spread(place, 32) == sub_k
        row = rows[t : t + 1, :]
        high = jnp.where(match_k, ((row >> 7) * 128).astype(F32), 0.0)
        low = jnp.where(match_k, (row & 127).astype(F32), 0.0)
        asked = jnp.concatenate(
            [jnp.concatenate([high, low], axis=1), nothing], axis=0
        ).astype(BF16)
        request = request + contract_lanes(jnp.concatenate([hot, hot], axis=1), asked)
        previous = prev_ref[t]
        truth = jnp.where(sub == lax.shift_right_logical(previous, 4), previous & 15, truth)
    request_ref[...] = jnp.where(lane == 32, truth, request.astype(I32))


def project_kernel(params_ref, out_ref, table_ref):
    def step(block, half):
        start = pl.multiple_of(half * 4096 + block * 1024, 1024)
        values = params_ref[:, pl.ds(start, 1024)].reshape(59, 8, 128)
        p = [values[i] for i in range(59)]
        (u, v, ca, cb, cc, opacity, ux, uy, uz) = geometry(p[:11])
        basis = harmonics(ux, uy, uz)
        colors = []
        for channel in range(3):
            color = 0.5 + basis[0] * p[11 + 16 * channel]
            for degree in range(1, 16):
                color = color + basis[degree] * p[11 + 16 * channel + degree]
            colors.append(color)
        for c, value in enumerate([u, v, ca, cb, cc] + colors + [opacity]):
            spot = pl.ds(pl.multiple_of(32 * c + 8 * block, 8), 8)
            table_ref[spot, 128 * half : 128 * half + 128] = value

    for half in range(2):
        lax.fori_loop(0, 4, lambda b, unused, half=half: (step(b, half), unused)[1], 0)
    for n, part in enumerate(split(table_ref[...], 3)):
        out_ref[288 * n : 288 * (n + 1), :] = part


def pick_kernel(
    asked_ref, table_ref, image_ref, out_ref, high_ref, low_ref, found_ref, stage_ref
):
    asked = asked_ref[...]
    index = asked.astype(F32).T[:32, :].astype(I32)
    high_ref[...] = (index >> 7) & 31
    low_ref[...] = (index & 127) + 128 * (index >> 12)
    sub_high = iota((32, 256), 0)
    sub_low = iota((256, 256), 0)
    for k in range(0, 32, 2):
        low = jnp.concatenate([low_ref[k : k + 1, :], low_ref[k + 1 : k + 2, :]], axis=1)
        high = jnp.concatenate([high_ref[k : k + 1, :], high_ref[k + 1 : k + 2, :]], axis=1)
        hot = indicator(spread(low, 256) == sub_low)
        parts = jnp.dot(table_ref[...], hot, preferred_element_type=F32)
        whole = parts[:288] + parts[288:576] + parts[576:]
        match = spread(high, 32) == sub_high
        for c in range(9):
            row = jnp.sum(
                jnp.where(match, whole[32 * c : 32 * c + 32], 0.0), axis=0, keepdims=True
            )
            found_ref[32 * c + k : 32 * c + k + 1, :] = row[:, :128]
            found_ref[32 * c + k + 1 : 32 * c + k + 2, :] = row[:, 128:]
    found_ref[288:, :] = jnp.zeros((96, 128), F32)
    truth = jnp.dot(
        indicator(asked[:, 32:33] == iota((128, 16), 1)), image_ref[...],
        preferred_element_type=F32,
    )
    for i in range(3):
        block = found_ref[128 * i : 128 * (i + 1), :].T
        for n, part in enumerate(split(block, 3)):
            stage_ref[pl.ds(3 * i + n, 128, stride=16), :] = part.astype(F32)
    for i in range(6):
        stage_ref[pl.ds(9 + i, 128, stride=16), :] = truth[:, 128 * i : 128 * (i + 1)]
    stage_ref[pl.ds(15, 128, stride=16), :] = jnp.zeros((128, 128), F32)
    out_ref[...] = stage_ref[...].astype(BF16)


def put_rows(out_ref, found_ref):
    for i in range(3):
        out_ref[pl.ds(i, 128, stride=4), :] = found_ref[128 * i : 128 * (i + 1), :].T
    out_ref[pl.ds(3, 128, stride=4), :] = jnp.zeros((128, 128), F32)


def swap_blocks(value):
    sub = iota((8, 128), 0)
    block = iota((8, 128), 1) >> 4
    for s in (4, 2, 1):
        up = pltpu.roll(pltpu.roll(value, 8 - s, 0), 16 * s, 1)
        down = up if s == 4 else pltpu.roll(pltpu.roll(value, s, 0), 128 - 16 * s, 1)
        sub_bit = sub & s
        block_bit = block & s
        value = jnp.where(
            sub_bit == block_bit, value, jnp.where(sub_bit < block_bit, up, down)
        )
    return value


def loss_and_slopes(images, target):
    loss = jnp.zeros((16, 1), F32)
    slopes = []
    for k in range(3):
        image = images[k]
        wanted = target[:, 256 * k : 256 * (k + 1)]
        difference = image - wanted
        smooth = jnp.sqrt(difference * difference + 0.0001)
        mean_r = jnp.sum(image, axis=1, keepdims=True) / 256.0
        mean_t = jnp.sum(wanted, axis=1, keepdims=True) / 256.0
        centered_r = image - mean_r
        centered_t = wanted - mean_t
        var_r = jnp.sum(centered_r * centered_r, axis=1, keepdims=True) / 256.0
        var_t = jnp.sum(centered_t * centered_t, axis=1, keepdims=True) / 256.0
        cov = jnp.sum(centered_r * centered_t, axis=1, keepdims=True) / 256.0
        top_m = 2.0 * mean_r * mean_t + 0.0001
        top_c = 2.0 * cov + 0.0009
        low_m = mean_r * mean_r + mean_t * mean_t + 0.0001
        low_v = var_r + var_t + 0.0009
        below = 1.0 / (low_m * low_v)
        similarity = top_m * top_c * below
        loss = loss + (0.8 / 3.0) * jnp.sum(smooth, axis=1, keepdims=True)
        loss = loss + (0.2 * 256.0 / 3.0) * (1.0 - similarity)
        by_mean = 2.0 * mean_t * top_c * below - similarity * 2.0 * mean_r / low_m
        by_cov = 2.0 * top_m * below
        by_var = -similarity / low_v
        slopes.append(
            (0.8 / 3.0) * difference / smooth
            - (0.2 / 3.0) * (by_mean + 2.0 * by_var * centered_r + by_cov * centered_t)
        )
    return loss, slopes


def render_kernel(
    arrived_ref, holder_ref, place_ref, tile_ref, prev_ref,
    picture_ref, loss_ref, out_ref, stage_ref,
    ordered_ref, row_ref, dx_ref, alpha_ref, weight_ref, reach_ref, moment_ref, found_ref,
):
    stage_ref[...] = arrived_ref[...].astype(F32)
    came = [stage_ref[pl.ds(i, 128, stride=16), :] for i in range(15)]
    table = [(came[3 * i] + came[3 * i + 1] + came[3 * i + 2]).T for i in range(3)]
    folded = []
    for c in range(9):
        part = table[c // 4][32 * (c % 4) : 32 * (c % 4) + 32, :]
        folded.append(jnp.concatenate([part[:16], part[16:]], axis=1))
    pieces = jnp.concatenate(split(jnp.concatenate(folded, axis=0), 3), axis=0)
    sub_slot = iota((256, 256), 0)
    sub_place = iota((16, 256), 0)
    for t in range(0, 16, 2):
        holder = jnp.concatenate([holder_ref[t : t + 1, :], holder_ref[t + 1 : t + 2, :]], axis=1)
        place = jnp.concatenate([place_ref[t : t + 1, :], place_ref[t + 1 : t + 2, :]], axis=1)
        hot = indicator(spread((place >> 4) * 128 + holder, 256) == sub_slot)
        parts = jnp.dot(pieces, hot, preferred_element_type=F32)
        whole = parts[:144] + parts[144:288] + parts[288:]
        match = spread(place & 15, 16) == sub_place
        for c in range(9):
            row = jnp.sum(
                jnp.where(match, whole[16 * c : 16 * c + 16], 0.0), axis=0, keepdims=True
            )
            ordered_ref[16 * c + t : 16 * c + t + 1, :] = row[:, :128]
            ordered_ref[16 * c + t + 1 : 16 * c + t + 2, :] = row[:, 128:]
    sub = iota((16, 128), 0)
    base_x = jnp.zeros((16, 128), F32)
    base_y = jnp.zeros((16, 128), F32)
    source = jnp.zeros((16, 128), I32)
    for t in range(16):
        number = tile_ref[t]
        tile_row = number // TW
        tile_column = number - tile_row * TW
        base_x = jnp.where(sub == t, (16 * tile_column + 8).astype(F32), base_x)
        base_y = jnp.where(sub == t, (16 * tile_row + 8).astype(F32), base_y)
        source = jnp.where(sub == t, lax.shift_right_logical(prev_ref[t], 4), source)
    ordered_ref[0:16, :] = ordered_ref[0:16, :] - base_x
    ordered_ref[16:32, :] = ordered_ref[16:32, :] - base_y
    ordered_ref[144:, :] = jnp.zeros((112, 128), F32)
    turned = [ordered_ref[0:128, :].T, ordered_ref[128:256, :].T]
    lane = iota((128, 128), 1)
    grid_x = (lane & 15).astype(F32) - 7.5
    for g in range(2):
        owner = (lane >> 4) + 8 * g

        def wide(c):
            return take_lane(turned[c // 8], owner + 16 * (c % 8))

        dx = grid_x - wide(0)
        dx_ref[g] = dx
        row_ref[g, 0] = (-0.5 * LOG2E) * wide(2) * dx * dx
        row_ref[g, 1] = (-LOG2E) * wide(3) * dx
        row_ref[g, 2] = (-0.5 * LOG2E) * wide(4)
        row_ref[g, 3] = wide(1)
        row_ref[g, 4] = wide(8)
        row_ref[g, 5] = wide(5)
        row_ref[g, 6] = wide(6)
        row_ref[g, 7] = wide(7)
    sub8 = iota((8, 128), 0)
    grid_y = [sub8.astype(F32) - 7.5, sub8.astype(F32) + 0.5]
    ones = jnp.ones((8, 128), F32)
    zero = jnp.zeros((8, 128), F32)

    def row_of(g, r, j):
        return spread(row_ref[g, r, pl.ds(j, 1), :], 8)

    def forward(j, state):
        reach = list(state[0])
        sums = list(state[1])
        for g in range(2):
            (part_a, part_b, part_c, gv, go, g0, g1, g2) = [row_of(g, r, j) for r in range(8)]
            for h in range(2):
                n = 2 * g + h
                dy = grid_y[h] - gv
                fall = jnp.exp2(part_a + dy * (part_b + part_c * dy))
                alpha = go * fall
                weight = alpha * reach[n]
                alpha_ref[j, n] = alpha
                weight_ref[j, n] = weight
                reach_ref[j, n] = fall * reach[n]
                reach[n] = reach[n] - weight
                sums[3 * n] = sums[3 * n] + weight * g0
                sums[3 * n + 1] = sums[3 * n + 1] + weight * g1
                sums[3 * n + 2] = sums[3 * n + 2] + weight * g2
        return (tuple(reach), tuple(sums))

    unused, sums = lax.fori_loop(
        0, 128, forward, (tuple([ones] * 4), tuple([zero] * 12)), unroll=4
    )
    chosen = indicator(source == iota((16, 128), 1))
    target = jnp.concatenate(
        [
            jnp.dot(chosen, came[9 + i].astype(BF16), preferred_element_type=F32)
            for i in range(6)
        ],
        axis=1,
    )
    images = []
    for k in range(3):
        image = jnp.concatenate(
            [
                jnp.concatenate(
                    [swap_blocks(sums[6 * g + k]), swap_blocks(sums[6 * g + 3 + k])], axis=1
                )
                for g in range(2)
            ],
            axis=0,
        )
        picture_ref[:, 256 * k : 256 * (k + 1)] = image
        images.append(image)
    loss, slopes = loss_and_slopes(images, target)
    loss_ref[...] = jnp.broadcast_to(loss, (16, 128))
    slope = [
        [
            swap_blocks(slopes[k][8 * g : 8 * g + 8, 128 * h : 128 * h + 128])
            for k in range(3)
        ]
        for g in range(2)
        for h in range(2)
    ]
    grid_yy = [grid_y[h] * grid_y[h] for h in range(2)]

    def fold(first, second, distance):
        bit = (sub8 & distance) != 0
        if distance == 4:
            return jnp.where(bit, second, first) + pltpu.roll(
                jnp.where(bit, first, second), 4, 0
            )
        return jnp.where(
            bit,
            second + pltpu.roll(second, distance, 0),
            first + pltpu.roll(first, 8 - distance, 0),
        )

    def backward(block, state):
        behind = list(state)
        base = pl.multiple_of(120 - 8 * block, 8)
        for g in range(2):
            waiting = {}
            for s in range(7, -1, -1):
                j = base + s
                (g0, g1, g2) = [row_of(g, r, j) for r in (5, 6, 7)]
                pulls = []
                shares = []
                for h in range(2):
                    n = 2 * g + h
                    value = slope[n][0] * g0 + slope[n][1] * g1 + slope[n][2] * g2
                    gap = value - behind[n]
                    pulls.append(reach_ref[j, n] * gap)
                    behind[n] = behind[n] + alpha_ref[j, n] * gap
                    weight = weight_ref[j, n]
                    shares.append([weight * slope[n][k] for k in range(3)])
                found = [
                    pulls[0] + pulls[1],
                    pulls[0] * grid_y[0] + pulls[1] * grid_y[1],
                    pulls[0] * grid_yy[0] + pulls[1] * grid_yy[1],
                    shares[0][0] + shares[1][0],
                    shares[0][1] + shares[1][1],
                    shares[0][2] + shares[1][2],
                ]
                spot = s
                for distance in (1, 2, 4):
                    if spot & distance:
                        break
                    above = waiting.pop((distance, spot + distance))
                    found = [fold(a, b, distance) for a, b in zip(found, above)]
                    if distance == 4:
                        for q in range(6):
                            moment_ref[g, q, pl.ds(base, 8), :] = found[q]
                else:
                    continue
                waiting[(distance, spot)] = found
        return tuple(behind)

    lax.fori_loop(0, 16, backward, tuple([zero] * 4))
    totals = jnp.zeros((16, 1152), F32)
    for g in range(2):
        dx = dx_ref[g]
        gv = row_ref[g, 3]
        m0 = moment_ref[g, 0]
        m1 = moment_ref[g, 1]
        sx = dx * m0
        sy = m1 - gv * m0
        syy = moment_ref[g, 2] - gv * (m1 + sy)
        stack = jnp.concatenate(
            [m0, sx, sy, dx * sx, dx * sy, syy]
            + [moment_ref[g, q] for q in range(3, 6)],
            axis=0,
        )
        tile = iota((16, 256), 0)
        pick = indicator(tile == ((iota((16, 256), 1) >> 4) & 7) + 8 * g)
        totals = totals + contract_lanes(pick, jnp.concatenate(split(stack, 2), axis=1))
    (m0, sx, sy, sxx, sxy, syy, d_red, d_green, d_blue) = [
        totals[:, 128 * c : 128 * c + 128] for c in range(9)
    ]
    (ca, cb, cc) = [ordered_ref[16 * c : 16 * c + 16, :] for c in (2, 3, 4)]
    opacity = ordered_ref[128:144, :]
    results = [
        opacity * (ca * sx + cb * sy),
        opacity * (cb * sx + cc * sy),
        -0.5 * opacity * sxx,
        -opacity * sxy,
        -0.5 * opacity * syy,
        d_red,
        d_green,
        d_blue,
        m0,
    ]
    parts = [[part.astype(F32) for part in split(result, 2)] for result in results]
    sub_k = iota((32, 128), 0)
    sub_h = iota((128, 128), 0)
    total = jnp.zeros((288, 128), F32)
    for t in range(0, 16, 2):
        hot = []
        left = [[], []]
        for tile in (t, t + 1):
            hot.append(indicator(spread(holder_ref[tile : tile + 1, :], 128) == sub_h))
            match = spread(place_ref[tile : tile + 1, :], 32) == sub_k
            for p in range(2):
                left[p].append(
                    jnp.concatenate(
                        [
                            jnp.where(match, parts[c][p][tile : tile + 1, :], 0.0)
                            for c in range(9)
                        ],
                        axis=0,
                    ).astype(BF16)
                )
        hot = jnp.concatenate(hot, axis=1)
        for p in range(2):
            total = total + contract_lanes(jnp.concatenate(left[p], axis=1), hot)
    found_ref[0:288, :] = total
    found_ref[288:, :] = jnp.zeros((96, 128), F32)
    put_rows(out_ref, found_ref)


def update_kernel(returned_ref, asked_ref, params_ref, out_ref, high_ref, low_ref, piece_ref, sum_ref):
    index = asked_ref[...].astype(F32).T[:32, :].astype(I32)
    high_ref[...] = (index >> 7) & 31
    low_ref[...] = (index & 127) + 128 * (index >> 12)
    for i in range(3):
        block = returned_ref[pl.ds(i, 128, stride=4), :].T
        rows = 128 if i < 2 else 32
        block = block[:rows, :]
        upper = block.astype(BF16).astype(F32)
        piece_ref[0, 128 * i : 128 * i + rows, :] = upper
        piece_ref[1, 128 * i : 128 * i + rows, :] = block - upper
    sum_ref[...] = jnp.zeros((288, 256), F32)
    sub_high = iota((32, 128), 0)
    sub_low = iota((256, 128), 0)

    def scatter(pair, unused):
        right = []
        left = [[], []]
        for half in range(2):
            k = 2 * pair + half
            low = jnp.broadcast_to(low_ref[pl.ds(k, 1), :], (256, 128))
            right.append(jnp.where(low == sub_low, 1.0, 0.0).astype(BF16))
            high = jnp.broadcast_to(high_ref[pl.ds(k, 1), :], (32, 128)) == sub_high
            for p in range(2):
                left[p].append(
                    jnp.concatenate(
                        [
                            jnp.where(high, piece_ref[p, pl.ds(32 * c + k, 1), :], 0.0)
                            for c in range(9)
                        ],
                        axis=0,
                    ).astype(BF16)
                )
        right = jnp.concatenate(right, axis=1)
        total = sum_ref[...]
        for p in range(2):
            total = total + lax.dot_general(
                jnp.concatenate(left[p], axis=1), right,
                (((1,), (1,)), ((), ())), preferred_element_type=F32,
            )
        sum_ref[...] = total
        return unused

    lax.fori_loop(0, 16, scatter, 0, unroll=16)

    def pull(block, half):
        start = pl.multiple_of(half * 4096 + block * 1024, 1024)
        values = params_ref[:, pl.ds(start, 1024)].reshape(59, 8, 128)
        p = [values[i] for i in range(59)]
        g = [
            sum_ref[pl.ds(pl.multiple_of(32 * c + 8 * block, 8), 8), 128 * half : 128 * half + 128]
            for c in range(9)
        ]
        primal, pull_geometry = jax.vjp(lambda *a: geometry(a), *p[:11])
        basis, pull_basis = jax.vjp(lambda *a: tuple(harmonics(*a)), *primal[6:9])
        d_basis = tuple(
            g[5] * p[11 + i] + g[6] * p[27 + i] + g[7] * p[43 + i] for i in range(16)
        )
        d_unit = pull_basis(d_basis)
        d_first = pull_geometry((g[0], g[1], g[2], g[3], g[4], g[8]) + tuple(d_unit))
        rows = list(d_first) + [g[5 + k] * basis[i] for k in range(3) for i in range(16)]
        out_ref[:, pl.ds(start, 1024)] = jnp.stack(rows, axis=0).reshape(59, 1024)

    for half in range(2):
        lax.fori_loop(0, 4, lambda b, unused, half=half: (pull(b, half), unused)[1], 0)


def vmem():
    return pl.BlockSpec(memory_space=pltpu.VMEM)


def smem():
    return pl.BlockSpec(memory_space=pltpu.SMEM)


def shape(dims, dtype=F32):
    return jax.ShapeDtypeStruct(dims, dtype)


ROOM = pltpu.CompilerParams(vmem_limit_bytes=40 * 1024 * 1024)


def swap(values):
    return lax.all_to_all(values, "dev", split_axis=0, concat_axis=0, tiled=True)


def swap_rows(values, rows):
    return swap(values.reshape(128, rows, 128)).reshape(128 * rows, 128)


def body(
    params, entry_shard, entry_row, depth_order, live_count, tile_of_slot, prev_slot, gt_image
):
    request, holder, place = pl.pallas_call(
        route_kernel,
        out_shape=(shape((128, 128), I32), shape((16, 128), I32), shape((16, 128), I32)),
        in_specs=[pl.BlockSpec(memory_space=pl.ANY)] * 5,
        out_specs=(vmem(),) * 3,
        scratch_shapes=[pltpu.VMEM((16, 128), I32)] * 3
        + [pltpu.SMEM((16,), I32)] * 2
        + [pltpu.SemaphoreType.DMA((5,))],
        compiler_params=pltpu.CompilerParams(vmem_limit_bytes=58 * 1024 * 1024),
        name="route",
    )(entry_shard, entry_row, depth_order, live_count, prev_slot)
    asked = swap(request)
    table = pl.pallas_call(
        project_kernel,
        out_shape=shape((864, 256), BF16),
        in_specs=[vmem()],
        out_specs=vmem(),
        scratch_shapes=[pltpu.VMEM((288, 256), F32)],
        compiler_params=ROOM,
        cost_estimate=pl.CostEstimate(
            flops=20_000_000, bytes_accessed=20_000_000, transcendentals=100_000
        ),
        name="project",
    )(params)
    picked = pl.pallas_call(
        pick_kernel,
        out_shape=shape((2048, 128), BF16),
        in_specs=[vmem(), vmem(), vmem()],
        out_specs=vmem(),
        scratch_shapes=[
            pltpu.VMEM((32, 128), I32),
            pltpu.VMEM((32, 128), I32),
            pltpu.VMEM((384, 128), F32),
            pltpu.VMEM((2048, 128), F32),
        ],
        compiler_params=ROOM,
        name="pick",
    )(asked, table, gt_image)
    arrived = swap_rows(picked, 16)
    picture, loss, outgoing = pl.pallas_call(
        render_kernel,
        out_shape=(shape((16, 768)), shape((16, 128)), shape((512, 128))),
        in_specs=[vmem()] * 3 + [smem(), smem()],
        out_specs=(vmem(),) * 3,
        scratch_shapes=[
            pltpu.VMEM((2048, 128), F32),
            pltpu.VMEM((256, 128), F32),
            pltpu.VMEM((2, 8, 128, 128), F32),
            pltpu.VMEM((2, 128, 128), F32),
            pltpu.VMEM((128, 4, 8, 128), F32),
            pltpu.VMEM((128, 4, 8, 128), F32),
            pltpu.VMEM((128, 4, 8, 128), F32),
            pltpu.VMEM((2, 6, 128, 128), F32),
            pltpu.VMEM((384, 128), F32),
        ],
        compiler_params=ROOM,
        name="render",
    )(arrived, holder, place, tile_of_slot, prev_slot)
    returned = swap_rows(outgoing, 4)
    gradients = pl.pallas_call(
        update_kernel,
        out_shape=shape((59, 8192)),
        in_specs=[vmem()] * 3,
        out_specs=vmem(),
        scratch_shapes=[
            pltpu.VMEM((32, 128), I32),
            pltpu.VMEM((32, 128), I32),
            pltpu.VMEM((2, 288, 128), F32),
            pltpu.VMEM((288, 256), F32),
        ],
        compiler_params=ROOM,
        name="update",
    )(returned, asked, params)
    return (gradients, picture, loss[:, 0])


def solution(mesh):
    return jax.shard_map(
        body,
        mesh=mesh,
        in_specs=(
            P(None, "dev"),
            P("dev", None),
            P("dev", None),
            P("dev", None),
            P("dev"),
            P("dev"),
            P("dev"),
            P("dev", None),
        ),
        out_specs=(P(None, "dev"), P("dev", None), P("dev")),
        check_vma=False,
    )
```

time: 121 us -> 74.1 us (0.61)
  Pallas kernels: 48.5 us -> 19.4 us
  local copies, waits for them, and re-layouts: 9.53 us -> 2.24 us
  waiting for transfers between devices: 21.1 us -> 17.4 us
  starting transfers between devices: 19 us -> 16.1 us
  blocking collectives: 20.7 us -> 18 us
    pallas_call x1, Pallas kernels: 28.9 us -> 9.58 us  [body(): pl.pallas_call(render_kernel, out_shape=(shape((16, 768)), shape((16, 128...]
    pallas_call x3 -> x2, Pallas kernels: 8.65 us -> 3.17 us  [the longest x1 2.46 us: body(): pl.pallas_call(pick_kernel, out_shape=shape((2048, 128), BF16), in_specs=...]
    unnamed x23 -> x14, local copies, waits for them, and re-layouts: 6.63 us -> 1.61 us
    all_to_all x3 -> x2, waiting for transfers between devices: 21.1 us -> 17.4 us  [swap(): lax.all_to_all(values, 'dev', split_axis=0, concat_axis=0, tiled=True)]
    pallas_call x1, Pallas kernels: 7.26 us -> 4.21 us  [body(): pl.pallas_call(update_kernel, out_shape=shape((59, 8192)), in_specs=[vmem...]
    all_to_all x3 -> x2, starting transfers between devices: 19 us -> 16.1 us  [swap(): lax.all_to_all(values, 'dev', split_axis=0, concat_axis=0, tiled=True)]
    all_to_all x1, blocking collectives: 20.7 us -> 18 us  [swap(): lax.all_to_all(values, 'dev', split_axis=0, concat_axis=0, tiled=True)]
    all_to_all x5 -> x0, local copies, waits for them, and re-layouts: 2.27 us -> none  [swap(): lax.all_to_all(values, 'dev', split_axis=0, concat_axis=0, tiled=True)]
  transfers between devices with their start and end apart: 3 -> 2, of which waited for: 2 -> 2; matrix products, arithmetic and copies ran while one was open for 1% -> 1% of each run, Pallas kernels for 7% -> 1%
where the time goes in v1:
time: 74.1 us; the launch traced here: 73.8 us
  Pallas kernels  19.4 us (26%)
  blocking collectives  18 us (24%)
  waiting for transfers between devices  17.4 us (23%)
  starting transfers between devices  16.1 us (22%)
  local copies, waits for them, and re-layouts  2.24 us (3%)
    all_to_all x1, blocking collectives, swap(): lax.all_to_all(values, 'dev', split_axis=0, concat_axis=0, tiled=True)  18 us
    all_to_all x2, waiting for transfers between devices, swap(): lax.all_to_all(values, 'dev', split_axis=0, concat_axis=0, tiled=True)  17.4 us
    all_to_all x2, starting transfers between devices, swap(): lax.all_to_all(values, 'dev', split_axis=0, concat_axis=0, tiled=True)  16.1 us
    pallas_call x1, Pallas kernels, body(): pl.pallas_call(render_kernel, out_shape=(shape((16, 768)), shape((16, 128...  9.58 us
    pallas_call x1, Pallas kernels, body(): pl.pallas_call(update_kernel, out_shape=shape((59, 8192)), in_specs=[vmem...  4.21 us
    pallas_call x1, Pallas kernels, body(): pl.pallas_call(pick_kernel, out_shape=shape((2048, 128), BF16), in_specs=...  2.46 us
    pallas_call x1, Pallas kernels, body(): pl.pallas_call(route_kernel, out_shape=(shape((128, 128), I32), shape((16...  2.42 us
    unnamed x14, local copies, waits for them, and re-layouts  1.61 us
  transfers between devices with their start and end apart: 2, of which 2 were waited for; matrix products, arithmetic and copies ran while one was open for 1% of the time, Pallas kernels for 1%

profile of v1, /device:TPU:1, one launch (start us, length us, event | category | flops | bytes accessed | tf_op | source)
XLA Modules:
  0.0 73.8 jit_solution(11043910208539614114)
XLA Ops:
  0.6 0.0 copy-start.2
  0.6 2.4 %route.1 = (s32[128,128]{1,0:T(8,128)}, s32[16,128]{1,0:T(8,128)}, s32[16,128]{1,0:T(8,128)}) custom-call(s32[16,128]{1,0:T(8,128)} %shard_hbm.1, s32[16,128]{1,0:T(8,128)} %row_hbm.1, s32[16,128]{1,0:T(8,128)} %order_hbm.1, s32[16]{0:T(128)} %live_hbm.1, s32[16]{0:T(128)} %prev_ref.1), custom_call_target="tpu_custom_call" | custom-call | tf_op jit(solution)/shard_map/route/pallas_call | solution.py:626
  3.1 11.5 %all-to-all-start = ((s32[128,1,128]{2,1,0:T(1,128)}), s32[128,1,128]{2,1,0:T(1,128)S(1)}, u32[]{:S(2)}, u32[]{:S(2)}) async-start(s32[128,1,128]{2,1,0:T(1,128)} %bitcast.13), calls=%async_computation | async-start | bytes 131072 | tf_op jit(solution)/shard_map/all_to_all | solution.py:616
  14.6 0.0 copy-start
  14.6 1.6 %copy-done = f32[59,8192]{1,0:T(8,128)S(1)} copy-done((f32[59,8192]{1,0:T(8,128)S(1)}, f32[59,8192]{1,0:T(8,128)}, u32[]{:S(2)}) %copy-start) | copy-done | bytes 1933336
  16.2 0.0 copy-start.3
  16.2 0.0 copy-start.4
  16.2 0.0 copy-start.5
  16.2 0.0 copy-start.6
  16.2 0.7 project.1.table_ref
  16.9 0.0 copy-start.1
  16.9 7.0 %all-to-all-done = s32[128,1,128]{2,1,0:T(1,128)S(1)} async-done(((s32[128,1,128]{2,1,0:T(1,128)}), s32[128,1,128]{2,1,0:T(1,128)S(1)}, u32[]{:S(2)}, u32[]{:S(2)}) %all-to-all-start) | async-done | bytes 65568 | tf_op jit(solution)/shard_map/all_to_all | solution.py:616
  23.9 0.0 copy-done.2
  23.9 2.5 %pick.1 = bf16[2048,128]{1,0:T(8,128)(2,1)S(1)} custom-call(s32[128,128]{1,0:T(8,128)S(1)} %bitcast.11, bf16[864,256]{1,0:T(8,128)(2,1)S(1)} %project.1.table_ref, bf16[16,768]{1,0:T(8,128)(2,1)S(1)} %copy-done.2), custom_call_target="tpu_custom_call" | custom-call | tf_op jit(solution)/shard_map/pick/pallas_call | solution.py:650
  26.4 18.0 %all_to_all.21 = bf16[128,16,128]{2,1,0:T(8,128)(2,1)S(1)} all-to-all(bf16[128,16,128]{2,1,0:T(8,128)(2,1)S(1)} %bitcast.9), channel_id=1, replica_groups=mesh['dev'=128] {'dev'}, dimensions={0} | all-to-all | bytes 1048576 | tf_op jit(solution)/shard_map/all_to_all | solution.py:616
  44.4 0.0 copy-done.3
  44.4 0.0 copy-done.4
  44.4 0.0 copy-done.5
  44.4 0.0 copy-done.6
  44.4 9.6 %render.1 = (f32[16,768]{1,0:T(8,128)}, f32[16,128]{1,0:T(8,128)S(1)}, f32[512,128]{1,0:T(8,128)}) custom-call(bf16[2048,128]{1,0:T(8,128)(2,1)S(1)} %bitcast.8, s32[16,128]{1,0:T(8,128)S(1)} %copy-done.3, s32[16,128]{1,0:T(8,128)S(1)} %copy-done.4, s32[16]{0:T(128)S(1)} %copy-done.6, s32[16]{0:T(128)S(1)} %copy-done.5), custom_call_target="tpu_custom_call" | custom-call | tf_op jit(solution)/shard_map/render/pallas_call | solution.py:665
  54.0 4.6 %all-to-all-start.2 = ((f32[128,4,128]{2,1,0:T(4,128)}), f32[128,4,128]{2,1,0:T(4,128)S(1)}, u32[]{:S(2)}, u32[]{:S(2)}) async-start(f32[128,4,128]{2,1,0:T(4,128)} %bitcast.5), calls=%async_computation.2 | async-start | bytes 524288 | tf_op jit(solution)/shard_map/all_to_all | solution.py:616
  58.6 0.6 slice_reduce_fusion
  59.2 10.4 %all-to-all-done.2 = f32[128,4,128]{2,1,0:T(4,128)S(1)} async-done(((f32[128,4,128]{2,1,0:T(4,128)}), f32[128,4,128]{2,1,0:T(4,128)S(1)}, u32[]{:S(2)}, u32[]{:S(2)}) %all-to-all-start.2) | async-done | bytes 262176 | tf_op jit(solution)/shard_map/all_to_all | solution.py:616
  69.6 0.0 copy-done.1
  69.6 4.2 %update.1 = f32[59,8192]{1,0:T(8,128)} custom-call(f32[512,128]{1,0:T(8,128)S(1)} %bitcast.10, s32[128,128]{1,0:T(8,128)S(1)} %bitcast.12, f32[59,8192]{1,0:T(8,128)S(1)} %copy-done.1), custom_call_target="tpu_custom_call" | custom-call | tf_op jit(solution)/shard_map/update/pallas_call | solution.py:685
Async XLA Ops:
  0.6 23.3 %copy-start.2 = (bf16[16,768]{1,0:T(8,128)(2,1)S(1)}, bf16[16,768]{1,0:T(8,128)(2,1)}, u32[]{:S(2)}) copy-start(bf16[16,768]{1,0:T(8,128)(2,1)} %image_ref.1) | copy-start | bytes 73732
  3.1 20.8 %all-to-all-start = ((s32[128,1,128]{2,1,0:T(1,128)}), s32[128,1,128]{2,1,0:T(1,128)S(1)}, u32[]{:S(2)}, u32[]{:S(2)}) async-start(s32[128,1,128]{2,1,0:T(1,128)} %bitcast.13), calls=%async_computation | async-start | bytes 131072 | tf_op jit(solution)/shard_map/all_to_all | solution.py:616
  14.6 1.6 %copy-start = (f32[59,8192]{1,0:T(8,128)S(1)}, f32[59,8192]{1,0:T(8,128)}, u32[]{:S(2)}) copy-start(f32[59,8192]{1,0:T(8,128)} %params_ref.3) | copy-start | bytes 5799940
  16.2 28.2 %copy-start.3 = (s32[16,128]{1,0:T(8,128)S(1)}, s32[16,128]{1,0:T(8,128)}, u32[]{:S(2)}) copy-start(s32[16,128]{1,0:T(8,128)} %get-tuple-element.10.holder_ref) | copy-start | bytes 24580
  16.2 28.2 %copy-start.4 = (s32[16,128]{1,0:T(8,128)S(1)}, s32[16,128]{1,0:T(8,128)}, u32[]{:S(2)}) copy-start(s32[16,128]{1,0:T(8,128)} %get-tuple-element.11.place_ref) | copy-start | bytes 24580
  16.2 28.2 %copy-start.5 = (s32[16]{0:T(128)S(1)}, s32[16]{0:T(128)}, u32[]{:S(2)}) copy-start(s32[16]{0:T(128)} %prev_ref.1) | copy-start | bytes 196
  16.2 28.2 %copy-start.6 = (s32[16]{0:T(128)S(1)}, s32[16]{0:T(128)}, u32[]{:S(2)}) copy-start(s32[16]{0:T(128)} %tile_ref.1) | copy-start | bytes 196
  16.9 52.7 %copy-start.1 = (f32[59,8192]{1,0:T(8,128)S(1)}, f32[59,8192]{1,0:T(8,128)}, u32[]{:S(2)}) copy-start(f32[59,8192]{1,0:T(8,128)} %params_ref.3) | copy-start | bytes 5799940
  54.0 15.6 %all-to-all-start.2 = ((f32[128,4,128]{2,1,0:T(4,128)}), f32[128,4,128]{2,1,0:T(4,128)S(1)}, u32[]{:S(2)}, u32[]{:S(2)}) async-start(f32[128,4,128]{2,1,0:T(4,128)} %bitcast.5), calls=%async_computation.2 | async-start | bytes 524288 | tf_op jit(solution)/shard_map/all_to_all | solution.py:616

commit v2 on v1

--- a/solution.py
+++ b/solution.py
@@ -22,8 +22,7 @@
     return jnp.take_along_axis(table, index, axis=1, mode="promise_in_bounds")
 
 
-def geometry(values):
-    (pos_x, pos_y, depth, ls0, ls1, ls2, q0, q1, q2, q3, logit) = values
+def conic(pos_x, pos_y, depth, ls0, ls1, ls2, q0, q1, q2, q3):
     scales = [jnp.exp(ls0), jnp.exp(ls1), jnp.exp(ls2)]
     inverse_q = lax.rsqrt(q0 * q0 + q1 * q1 + q2 * q2 + q3 * q3)
     w_part = q0 * inverse_q
@@ -59,18 +58,12 @@
     spread_xy = first[0] * second[0] + first[1] * second[1] + first[2] * second[2]
     spread_yy = second[0] * second[0] + second[1] * second[1] + second[2] * second[2] + 0.3
     inverse_det = 1.0 / (spread_xx * spread_yy - spread_xy * spread_xy)
+    return (spread_yy * inverse_det, -spread_xy * inverse_det, spread_xx * inverse_det)
+
+
+def direction(pos_x, pos_y, depth):
     inverse_norm = lax.rsqrt(pos_x * pos_x + pos_y * pos_y + depth * depth)
-    return (
-        FOCAL * pos_x / depth + 8.0 * TW,
-        FOCAL * pos_y / depth + 8.0 * TH,
-        spread_yy * inverse_det,
-        -spread_xy * inverse_det,
-        spread_xx * inverse_det,
-        lax.logistic(logit),
-        pos_x * inverse_norm,
-        pos_y * inverse_norm,
-        depth * inverse_norm,
-    )
+    return (pos_x * inverse_norm, pos_y * inverse_norm, depth * inverse_norm)
 
 
 def harmonics(unit_x, unit_y, unit_z):
@@ -117,6 +110,12 @@
 
 def spread(row, count):
     return jnp.broadcast_to(row, (count, row.shape[1]))
+
+
+def pair_rows(ref, row, count):
+    return jnp.concatenate(
+        [spread(ref[pl.ds(row + n, 1), :], count) for n in range(2)], axis=1
+    )
 
 
 def route_kernel(
@@ -183,8 +182,11 @@
         start = pl.multiple_of(half * 4096 + block * 1024, 1024)
         values = params_ref[:, pl.ds(start, 1024)].reshape(59, 8, 128)
         p = [values[i] for i in range(59)]
-        (u, v, ca, cb, cc, opacity, ux, uy, uz) = geometry(p[:11])
-        basis = harmonics(ux, uy, uz)
+        (ca, cb, cc) = conic(*p[:10])
+        u = FOCAL * p[0] / p[2] + 8.0 * TW
+        v = FOCAL * p[1] / p[2] + 8.0 * TH
+        opacity = lax.logistic(p[10])
+        basis = harmonics(*direction(*p[:3]))
         colors = []
         for channel in range(3):
             color = 0.5 + basis[0] * p[11 + 16 * channel]
@@ -211,12 +213,10 @@
     sub_high = iota((32, 256), 0)
     sub_low = iota((256, 256), 0)
     for k in range(0, 32, 2):
-        low = jnp.concatenate([low_ref[k : k + 1, :], low_ref[k + 1 : k + 2, :]], axis=1)
-        high = jnp.concatenate([high_ref[k : k + 1, :], high_ref[k + 1 : k + 2, :]], axis=1)
-        hot = indicator(spread(low, 256) == sub_low)
+        hot = indicator(pair_rows(low_ref, k, 256) == sub_low)
         parts = jnp.dot(table_ref[...], hot, preferred_element_type=F32)
         whole = parts[:288] + parts[288:576] + parts[576:]
-        match = spread(high, 32) == sub_high
+        match = pair_rows(high_ref, k, 32) == sub_high
         for c in range(9):
             row = jnp.sum(
                 jnp.where(match, whole[32 * c : 32 * c + 32], 0.0), axis=0, keepdims=True
@@ -240,8 +240,7 @@
 
 def put_rows(out_ref, found_ref):
     for i in range(3):
-        out_ref[pl.ds(i, 128, stride=4), :] = found_ref[128 * i : 128 * (i + 1), :].T
-    out_ref[pl.ds(3, 128, stride=4), :] = jnp.zeros((128, 128), F32)
+        out_ref[pl.ds(i, 128, stride=3), :] = found_ref[128 * i : 128 * (i + 1), :].T
 
 
 def swap_blocks(value):
@@ -295,7 +294,10 @@
     arrived_ref, holder_ref, place_ref, tile_ref, prev_ref,
     picture_ref, loss_ref, out_ref, stage_ref,
     ordered_ref, row_ref, dx_ref, alpha_ref, weight_ref, reach_ref, moment_ref, found_ref,
+    code_ref, low_ref, part_ref,
 ):
+    code_ref[...] = (place_ref[...] >> 4) * 128 + holder_ref[...]
+    low_ref[...] = place_ref[...] & 15
     stage_ref[...] = arrived_ref[...].astype(F32)
     came = [stage_ref[pl.ds(i, 128, stride=16), :] for i in range(15)]
     table = [(came[3 * i] + came[3 * i + 1] + came[3 * i + 2]).T for i in range(3)]
@@ -306,19 +308,22 @@
     pieces = jnp.concatenate(split(jnp.concatenate(folded, axis=0), 3), axis=0)
     sub_slot = iota((256, 256), 0)
     sub_place = iota((16, 256), 0)
-    for t in range(0, 16, 2):
-        holder = jnp.concatenate([holder_ref[t : t + 1, :], holder_ref[t + 1 : t + 2, :]], axis=1)
-        place = jnp.concatenate([place_ref[t : t + 1, :], place_ref[t + 1 : t + 2, :]], axis=1)
-        hot = indicator(spread((place >> 4) * 128 + holder, 256) == sub_slot)
+
+    def pick(pair, unused):
+        t = 2 * pair
+        hot = indicator(pair_rows(code_ref, t, 256) == sub_slot)
         parts = jnp.dot(pieces, hot, preferred_element_type=F32)
         whole = parts[:144] + parts[144:288] + parts[288:]
-        match = spread(place & 15, 16) == sub_place
+        match = pair_rows(low_ref, t, 16) == sub_place
         for c in range(9):
             row = jnp.sum(
                 jnp.where(match, whole[16 * c : 16 * c + 16], 0.0), axis=0, keepdims=True
             )
-            ordered_ref[16 * c + t : 16 * c + t + 1, :] = row[:, :128]
-            ordered_ref[16 * c + t + 1 : 16 * c + t + 2, :] = row[:, 128:]
+            ordered_ref[pl.ds(16 * c + t, 1), :] = row[:, :128]
+            ordered_ref[pl.ds(16 * c + t + 1, 1), :] = row[:, 128:]
+        return unused
+
+    lax.fori_loop(0, 8, pick, 0, unroll=PICK_UNROLL)
     sub = iota((16, 128), 0)
     base_x = jnp.zeros((16, 128), F32)
     base_y = jnp.zeros((16, 128), F32)
@@ -381,7 +386,7 @@
         return (tuple(reach), tuple(sums))
 
     unused, sums = lax.fori_loop(
-        0, 128, forward, (tuple([ones] * 4), tuple([zero] * 12)), unroll=4
+        0, 128, forward, (tuple([ones] * 4), tuple([zero] * 12)), unroll=FORWARD_UNROLL
     )
     chosen = indicator(source == iota((16, 128), 1))
     target = jnp.concatenate(
@@ -502,21 +507,24 @@
         d_blue,
         m0,
     ]
-    parts = [[part.astype(F32) for part in split(result, 2)] for result in results]
+    for c, result in enumerate(results):
+        for p, part in enumerate(split(result, 2)):
+            part_ref[p, 16 * c : 16 * c + 16, :] = part.astype(F32)
     sub_k = iota((32, 128), 0)
     sub_h = iota((128, 128), 0)
-    total = jnp.zeros((288, 128), F32)
-    for t in range(0, 16, 2):
+
+    def give(pair, total):
         hot = []
         left = [[], []]
-        for tile in (t, t + 1):
-            hot.append(indicator(spread(holder_ref[tile : tile + 1, :], 128) == sub_h))
-            match = spread(place_ref[tile : tile + 1, :], 32) == sub_k
+        for n in range(2):
+            tile = 2 * pair + n
+            hot.append(indicator(spread(holder_ref[pl.ds(tile, 1), :], 128) == sub_h))
+            match = spread(place_ref[pl.ds(tile, 1), :], 32) == sub_k
             for p in range(2):
                 left[p].append(
                     jnp.concatenate(
                         [
-                            jnp.where(match, parts[c][p][tile : tile + 1, :], 0.0)
+                            jnp.where(match, part_ref[p, pl.ds(16 * c + tile, 1), :], 0.0)
                             for c in range(9)
                         ],
                         axis=0,
@@ -525,76 +533,112 @@
         hot = jnp.concatenate(hot, axis=1)
         for p in range(2):
             total = total + contract_lanes(jnp.concatenate(left[p], axis=1), hot)
+        return total
+
+    total = lax.fori_loop(0, 8, give, jnp.zeros((288, 128), F32), unroll=GIVE_UNROLL)
     found_ref[0:288, :] = total
     found_ref[288:, :] = jnp.zeros((96, 128), F32)
     put_rows(out_ref, found_ref)
 
 
-def update_kernel(returned_ref, asked_ref, params_ref, out_ref, high_ref, low_ref, piece_ref, sum_ref):
+def update_kernel(
+    returned_ref, asked_ref, params_ref, out_hbm,
+    high_ref, low_ref, piece_ref, sum_ref, out_ref, sems,
+):
     index = asked_ref[...].astype(F32).T[:32, :].astype(I32)
     high_ref[...] = (index >> 7) & 31
     low_ref[...] = (index & 127) + 128 * (index >> 12)
     for i in range(3):
-        block = returned_ref[pl.ds(i, 128, stride=4), :].T
+        block = returned_ref[pl.ds(i, 128, stride=3), :].T
         rows = 128 if i < 2 else 32
         block = block[:rows, :]
         upper = block.astype(BF16).astype(F32)
         piece_ref[0, 128 * i : 128 * i + rows, :] = upper
         piece_ref[1, 128 * i : 128 * i + rows, :] = block - upper
-    sum_ref[...] = jnp.zeros((288, 256), F32)
     sub_high = iota((32, 128), 0)
-    sub_low = iota((256, 128), 0)
-
-    def scatter(pair, unused):
-        right = []
+    sub_low = iota((256, 256), 0)
+
+    def scatter(pair, total):
+        k = 2 * pair
         left = [[], []]
-        for half in range(2):
-            k = 2 * pair + half
-            low = jnp.broadcast_to(low_ref[pl.ds(k, 1), :], (256, 128))
-            right.append(jnp.where(low == sub_low, 1.0, 0.0).astype(BF16))
-            high = jnp.broadcast_to(high_ref[pl.ds(k, 1), :], (32, 128)) == sub_high
+        for n in (k, k + 1):
+            match = spread(high_ref[pl.ds(n, 1), :], 32) == sub_high
             for p in range(2):
                 left[p].append(
                     jnp.concatenate(
                         [
-                            jnp.where(high, piece_ref[p, pl.ds(32 * c + k, 1), :], 0.0)
+                            jnp.where(match, piece_ref[p, pl.ds(32 * c + n, 1), :], 0.0)
                             for c in range(9)
                         ],
                         axis=0,
                     ).astype(BF16)
                 )
-        right = jnp.concatenate(right, axis=1)
-        total = sum_ref[...]
+        hot = indicator(pair_rows(low_ref, k, 256) == sub_low)
         for p in range(2):
-            total = total + lax.dot_general(
-                jnp.concatenate(left[p], axis=1), right,
-                (((1,), (1,)), ((), ())), preferred_element_type=F32,
-            )
-        sum_ref[...] = total
-        return unused
-
-    lax.fori_loop(0, 16, scatter, 0, unroll=16)
-
-    def pull(block, half):
-        start = pl.multiple_of(half * 4096 + block * 1024, 1024)
+            total = total + contract_lanes(jnp.concatenate(left[p], axis=1), hot)
+        return total
+
+    total = lax.fori_loop(0, 16, scatter, jnp.zeros((288, 256), F32), unroll=SCATTER_UNROLL)
+    sum_ref[0] = total[:, :128]
+    sum_ref[1] = total[:, 128:]
+    early = iota((8, 128), 0) < 3
+
+    def leave(block):
+        span = pl.ds(pl.multiple_of(block * 1024, 1024), 1024)
+        return pltpu.make_async_copy(out_ref.at[:, span], out_hbm.at[:, span], sems.at[block])
+
+    def pull(place, half):
+        block = place + 4 * half
+        start = pl.multiple_of(block * 1024, 1024)
         values = params_ref[:, pl.ds(start, 1024)].reshape(59, 8, 128)
         p = [values[i] for i in range(59)]
         g = [
-            sum_ref[pl.ds(pl.multiple_of(32 * c + 8 * block, 8), 8), 128 * half : 128 * half + 128]
-            for c in range(9)
+            sum_ref[half, pl.ds(pl.multiple_of(32 * c + 8 * place, 8), 8), :] for c in range(9)
         ]
-        primal, pull_geometry = jax.vjp(lambda *a: geometry(a), *p[:11])
-        basis, pull_basis = jax.vjp(lambda *a: tuple(harmonics(*a)), *primal[6:9])
+        unused_conic, pull_conic = jax.vjp(conic, *p[:10])
+        unit, pull_unit = jax.vjp(direction, *p[:3])
+        basis, pull_basis = jax.vjp(lambda *d: tuple(harmonics(*d)), *unit)
         d_basis = tuple(
             g[5] * p[11 + i] + g[6] * p[27 + i] + g[7] * p[43 + i] for i in range(16)
         )
-        d_unit = pull_basis(d_basis)
-        d_first = pull_geometry((g[0], g[1], g[2], g[3], g[4], g[8]) + tuple(d_unit))
-        rows = list(d_first) + [g[5 + k] * basis[i] for k in range(3) for i in range(16)]
-        out_ref[:, pl.ds(start, 1024)] = jnp.stack(rows, axis=0).reshape(59, 1024)
+        first = list(pull_conic((g[2], g[3], g[4])))
+        for i, slope in enumerate(pull_unit(pull_basis(d_basis))):
+            first[i] = first[i] + slope
+        focal_z = FOCAL / p[2]
+        opacity = lax.logistic(p[10])
+        first[0] = first[0] + g[0] * focal_z
+        first[1] = first[1] + g[1] * focal_z
+        first[2] = first[2] - focal_z * ((g[0] * p[0] + g[1] * p[1]) / p[2])
+        first.append(g[8] * (opacity * (1.0 - opacity)))
+        blank = jnp.zeros((8, 128), F32)
+
+        def turn(rows):
+            return jnp.stack(rows, axis=0).reshape(8, 1024)
+
+        out_ref[0:8, pl.ds(start, 1024)] = turn(first[:8])
+        rest = turn(first[8:] + [blank] * 5)
+        ends_all = turn([basis[i] for i in (13, 14, 15, 0, 1, 2, 3, 4)])
+        middle_all = turn([basis[i] for i in range(5, 13)])
+        for s in range(8):
+            column = pl.ds(pl.multiple_of(start + 128 * s, 128), 128)
+            ends = ends_all[:, 128 * s : 128 * s + 128]
+            middle = middle_all[:, 128 * s : 128 * s + 128]
+            (red, green, blue) = [
+                spread(sum_ref[half, pl.ds(32 * c + 8 * place + s, 1), :], 8) for c in (5, 6, 7)
+            ]
+            out_ref[8:16, column] = jnp.where(early, rest[:, 128 * s : 128 * s + 128], ends * red)
+            out_ref[16:24, column] = middle * red
+            out_ref[24:32, column] = ends * jnp.where(early, red, green)
+            out_ref[32:40, column] = middle * green
+            out_ref[40:48, column] = ends * jnp.where(early, green, blue)
+            out_ref[48:56, column] = middle * blue
+            out_ref[56:59, column] = (ends * blue)[:3]
+        leave(block).start()
 
     for half in range(2):
         lax.fori_loop(0, 4, lambda b, unused, half=half: (pull(b, half), unused)[1], 0)
+    for block in range(8):
+        leave(block).wait()
 
 
 def vmem():
@@ -605,10 +649,19 @@
     return pl.BlockSpec(memory_space=pltpu.SMEM)
 
 
+def anywhere():
+    return pl.BlockSpec(memory_space=pl.ANY)
+
+
 def shape(dims, dtype=F32):
     return jax.ShapeDtypeStruct(dims, dtype)
 
 
+PICK_UNROLL = 4
+FORWARD_UNROLL = 4
+SCATTER_UNROLL = 16
+GIVE_UNROLL = 4
+WIDE = pltpu.CompilerParams(vmem_limit_bytes=58 * 1024 * 1024)
 ROOM = pltpu.CompilerParams(vmem_limit_bytes=40 * 1024 * 1024)
 
 
@@ -626,12 +679,12 @@
     request, holder, place = pl.pallas_call(
         route_kernel,
         out_shape=(shape((128, 128), I32), shape((16, 128), I32), shape((16, 128), I32)),
-        in_specs=[pl.BlockSpec(memory_space=pl.ANY)] * 5,
+        in_specs=[anywhere()] * 5,
         out_specs=(vmem(),) * 3,
         scratch_shapes=[pltpu.VMEM((16, 128), I32)] * 3
         + [pltpu.SMEM((16,), I32)] * 2
         + [pltpu.SemaphoreType.DMA((5,))],
-        compiler_params=pltpu.CompilerParams(vmem_limit_bytes=58 * 1024 * 1024),
+        compiler_params=WIDE,
         name="route",
     )(entry_shard, entry_row, depth_order, live_count, prev_slot)
     asked = swap(request)
@@ -664,7 +717,7 @@
     arrived = swap_rows(picked, 16)
     picture, loss, outgoing = pl.pallas_call(
         render_kernel,
-        out_shape=(shape((16, 768)), shape((16, 128)), shape((512, 128))),
+        out_shape=(shape((16, 768)), shape((16, 128)), shape((384, 128))),
         in_specs=[vmem()] * 3 + [smem(), smem()],
         out_specs=(vmem(),) * 3,
         scratch_shapes=[
@@ -677,21 +730,26 @@
             pltpu.VMEM((128, 4, 8, 128), F32),
             pltpu.VMEM((2, 6, 128, 128), F32),
             pltpu.VMEM((384, 128), F32),
+            pltpu.VMEM((16, 128), I32),
+            pltpu.VMEM((16, 128), I32),
+            pltpu.VMEM((2, 144, 128), F32),
         ],
         compiler_params=ROOM,
         name="render",
     )(arrived, holder, place, tile_of_slot, prev_slot)
-    returned = swap_rows(outgoing, 4)
+    returned = swap(outgoing.reshape(128, 1, 384)).reshape(384, 128)
     gradients = pl.pallas_call(
         update_kernel,
         out_shape=shape((59, 8192)),
-        in_specs=[vmem()] * 3,
-        out_specs=vmem(),
+        in_specs=[vmem(), vmem(), vmem()],
+        out_specs=anywhere(),
         scratch_shapes=[
             pltpu.VMEM((32, 128), I32),
             pltpu.VMEM((32, 128), I32),
             pltpu.VMEM((2, 288, 128), F32),
-            pltpu.VMEM((288, 256), F32),
+            pltpu.VMEM((2, 288, 128), F32),
+            pltpu.VMEM((59, 8192), F32),
+            pltpu.SemaphoreType.DMA((8,)),
         ],
         compiler_params=ROOM,
         name="update",

time: 74.1 us -> 72.4 us (0.977)
  Pallas kernels: 19.4 us -> 18.3 us
where the time goes in v2:
time: 72.4 us; the launch traced here: 72.1 us
  Pallas kernels  18.3 us (25%)
  blocking collectives  18 us (25%)
  waiting for transfers between devices  16.8 us (23%)
  starting transfers between devices  16.1 us (22%)
  local copies, waits for them, and re-layouts  2.24 us (3%)
    all_to_all x1, blocking collectives, swap(): lax.all_to_all(values, 'dev', split_axis=0, concat_axis=0, tiled=True)  18 us
    all_to_all x2, waiting for transfers between devices, swap(): lax.all_to_all(values, 'dev', split_axis=0, concat_axis=0, tiled=True)  16.8 us
    all_to_all x2, starting transfers between devices, swap(): lax.all_to_all(values, 'dev', split_axis=0, concat_axis=0, tiled=True)  16.1 us
    pallas_call x1, Pallas kernels, body(): pl.pallas_call(render_kernel, out_shape=(shape((16, 768)), shape((16, 128...  9.05 us
    pallas_call x1, Pallas kernels, body(): pl.pallas_call(update_kernel, out_shape=shape((59, 8192)), in_specs=[vmem...  3.61 us
    pallas_call x1, Pallas kernels, body(): pl.pallas_call(pick_kernel, out_shape=shape((2048, 128), BF16), in_specs=...  2.46 us
    pallas_call x1, Pallas kernels, body(): pl.pallas_call(route_kernel, out_shape=(shape((128, 128), I32), shape((16...  2.42 us
    unnamed x14, local copies, waits for them, and re-layouts  1.61 us
  transfers between devices with their start and end apart: 2, of which 2 were waited for; matrix products, arithmetic and copies ran while one was open for 1% of the time, Pallas kernels for 1%

profile of v2, /device:TPU:1, one launch (start us, length us, event | category | flops | bytes accessed | tf_op | source)
XLA Modules:
  0.0 72.1 jit_solution(3415842957419400014)
XLA Ops:
  0.6 0.0 copy-start.2
  0.6 2.4 %route.1 = (s32[128,128]{1,0:T(8,128)}, s32[16,128]{1,0:T(8,128)}, s32[16,128]{1,0:T(8,128)}) custom-call(s32[16,128]{1,0:T(8,128)} %shard_hbm.1, s32[16,128]{1,0:T(8,128)} %row_hbm.1, s32[16,128]{1,0:T(8,128)} %order_hbm.1, s32[16]{0:T(128)} %live_hbm.1, s32[16]{0:T(128)} %prev_ref.1), custom_call_target="tpu_custom_call" | custom-call | tf_op jit(solution)/shard_map/route/pallas_call | solution.py:679
  3.1 11.5 %all-to-all-start = ((s32[128,1,128]{2,1,0:T(1,128)}), s32[128,1,128]{2,1,0:T(1,128)S(1)}, u32[]{:S(2)}, u32[]{:S(2)}) async-start(s32[128,1,128]{2,1,0:T(1,128)} %bitcast.13), calls=%async_computation | async-start | bytes 131072 | tf_op jit(solution)/shard_map/all_to_all | solution.py:669
  14.6 0.0 copy-start
  14.6 1.6 %copy-done = f32[59,8192]{1,0:T(8,128)S(1)} copy-done((f32[59,8192]{1,0:T(8,128)S(1)}, f32[59,8192]{1,0:T(8,128)}, u32[]{:S(2)}) %copy-start) | copy-done | bytes 1933336
  16.2 0.0 copy-start.3
  16.2 0.0 copy-start.4
  16.2 0.0 copy-start.5
  16.2 0.0 copy-start.6
  16.2 0.7 project.1.table_ref
  16.9 0.0 copy-start.1
  16.9 7.0 %all-to-all-done = s32[128,1,128]{2,1,0:T(1,128)S(1)} async-done(((s32[128,1,128]{2,1,0:T(1,128)}), s32[128,1,128]{2,1,0:T(1,128)S(1)}, u32[]{:S(2)}, u32[]{:S(2)}) %all-to-all-start) | async-done | bytes 65568 | tf_op jit(solution)/shard_map/all_to_all | solution.py:669
  23.9 0.0 copy-done.2
  23.9 2.5 %pick.1 = bf16[2048,128]{1,0:T(8,128)(2,1)S(1)} custom-call(s32[128,128]{1,0:T(8,128)S(1)} %bitcast.11, bf16[864,256]{1,0:T(8,128)(2,1)S(1)} %project.1.table_ref, bf16[16,768]{1,0:T(8,128)(2,1)S(1)} %copy-done.2), custom_call_target="tpu_custom_call" | custom-call | tf_op jit(solution)/shard_map/pick/pallas_call | solution.py:703
  26.4 18.0 %all_to_all.21 = bf16[128,16,128]{2,1,0:T(8,128)(2,1)S(1)} all-to-all(bf16[128,16,128]{2,1,0:T(8,128)(2,1)S(1)} %bitcast.9), channel_id=1, replica_groups=mesh['dev'=128] {'dev'}, dimensions={0} | all-to-all | bytes 1048576 | tf_op jit(solution)/shard_map/all_to_all | solution.py:669
  44.4 0.0 copy-done.3
  44.4 0.0 copy-done.4
  44.4 0.0 copy-done.5
  44.4 0.0 copy-done.6
  44.4 9.0 %render.1 = (f32[16,768]{1,0:T(8,128)}, f32[16,128]{1,0:T(8,128)S(1)}, f32[384,128]{1,0:T(8,128)}) custom-call(bf16[2048,128]{1,0:T(8,128)(2,1)S(1)} %bitcast.8, s32[16,128]{1,0:T(8,128)S(1)} %copy-done.3, s32[16,128]{1,0:T(8,128)S(1)} %copy-done.4, s32[16]{0:T(128)S(1)} %copy-done.6, s32[16]{0:T(128)S(1)} %copy-done.5), custom_call_target="tpu_custom_call" | custom-call | tf_op jit(solution)/shard_map/render/pallas_call | solution.py:718
  53.4 4.6 %all-to-all-start.2 = ((f32[128,1,384]{2,1,0:T(1,128)}), f32[128,1,384]{2,1,0:T(1,128)S(1)}, u32[]{:S(2)}, u32[]{:S(2)}) async-start(f32[128,1,384]{2,1,0:T(1,128)} %bitcast.5), calls=%async_computation.2 | async-start | bytes 393216 | tf_op jit(solution)/shard_map/all_to_all | solution.py:669
  58.1 0.6 slice_reduce_fusion
  58.7 9.9 %all-to-all-done.2 = f32[128,1,384]{2,1,0:T(1,128)S(1)} async-done(((f32[128,1,384]{2,1,0:T(1,128)}), f32[128,1,384]{2,1,0:T(1,128)S(1)}, u32[]{:S(2)}, u32[]{:S(2)}) %all-to-all-start.2) | async-done | bytes 196640 | tf_op jit(solution)/shard_map/all_to_all | solution.py:669
  68.5 0.0 copy-done.1
  68.5 3.6 %update.1 = f32[59,8192]{1,0:T(8,128)} custom-call(f32[384,128]{1,0:T(8,128)S(1)} %bitcast.10, s32[128,128]{1,0:T(8,128)S(1)} %bitcast.12, f32[59,8192]{1,0:T(8,128)S(1)} %copy-done.1), custom_call_target="tpu_custom_call" | custom-call | tf_op jit(solution)/shard_map/update/pallas_call | solution.py:741
Async XLA Ops:
  0.6 23.3 %copy-start.2 = (bf16[16,768]{1,0:T(8,128)(2,1)S(1)}, bf16[16,768]{1,0:T(8,128)(2,1)}, u32[]{:S(2)}) copy-start(bf16[16,768]{1,0:T(8,128)(2,1)} %image_ref.1) | copy-start | bytes 73732
  3.1 20.8 %all-to-all-start = ((s32[128,1,128]{2,1,0:T(1,128)}), s32[128,1,128]{2,1,0:T(1,128)S(1)}, u32[]{:S(2)}, u32[]{:S(2)}) async-start(s32[128,1,128]{2,1,0:T(1,128)} %bitcast.13), calls=%async_computation | async-start | bytes 131072 | tf_op jit(solution)/shard_map/all_to_all | solution.py:669
  14.6 1.6 %copy-start = (f32[59,8192]{1,0:T(8,128)S(1)}, f32[59,8192]{1,0:T(8,128)}, u32[]{:S(2)}) copy-start(f32[59,8192]{1,0:T(8,128)} %params_ref.3) | copy-start | bytes 5799940
  16.2 28.2 %copy-start.3 = (s32[16,128]{1,0:T(8,128)S(1)}, s32[16,128]{1,0:T(8,128)}, u32[]{:S(2)}) copy-start(s32[16,128]{1,0:T(8,128)} %get-tuple-element.10.holder_ref) | copy-start | bytes 24580
  16.2 28.2 %copy-start.4 = (s32[16,128]{1,0:T(8,128)S(1)}, s32[16,128]{1,0:T(8,128)}, u32[]{:S(2)}) copy-start(s32[16,128]{1,0:T(8,128)} %get-tuple-element.11.place_ref) | copy-start | bytes 24580
  16.2 28.2 %copy-start.5 = (s32[16]{0:T(128)S(1)}, s32[16]{0:T(128)}, u32[]{:S(2)}) copy-start(s32[16]{0:T(128)} %prev_ref.1) | copy-start | bytes 196
  16.2 28.2 %copy-start.6 = (s32[16]{0:T(128)S(1)}, s32[16]{0:T(128)}, u32[]{:S(2)}) copy-start(s32[16]{0:T(128)} %tile_ref.1) | copy-start | bytes 196
  16.9 51.6 %copy-start.1 = (f32[59,8192]{1,0:T(8,128)S(1)}, f32[59,8192]{1,0:T(8,128)}, u32[]{:S(2)}) copy-start(f32[59,8192]{1,0:T(8,128)} %params_ref.3) | copy-start | bytes 5799940
  53.4 15.1 %all-to-all-start.2 = ((f32[128,1,384]{2,1,0:T(1,128)}), f32[128,1,384]{2,1,0:T(1,128)S(1)}, u32[]{:S(2)}, u32[]{:S(2)}) async-start(f32[128,1,384]{2,1,0:T(1,128)} %bitcast.5), calls=%async_computation.2 | async-start | bytes 393216 | tf_op jit(solution)/shard_map/all_to_all | solution.py:669

commit v3 on v2

--- a/solution.py
+++ b/solution.py
@@ -149,9 +149,8 @@
     counter = indicator((wide_lane >= 128) | (wide_row < wide_lane))
     sub_k = iota((32, 128), 0)
     carry = jnp.zeros((128, 128), F32)
-    request = jnp.zeros((128, 128), F32)
+    request = jnp.zeros((128, 32), F32)
     truth = jnp.zeros((128, 128), I32)
-    nothing = jnp.zeros((96, 256), F32)
     for t in range(tiles):
         live = order[t : t + 1, :] < live_ref[t]
         holder = jnp.where(live, shards[t : t + 1, :], -1)
@@ -168,13 +167,12 @@
         row = rows[t : t + 1, :]
         high = jnp.where(match_k, ((row >> 7) * 128).astype(F32), 0.0)
         low = jnp.where(match_k, (row & 127).astype(F32), 0.0)
-        asked = jnp.concatenate(
-            [jnp.concatenate([high, low], axis=1), nothing], axis=0
-        ).astype(BF16)
+        asked = jnp.concatenate([high, low], axis=1).astype(BF16)
         request = request + contract_lanes(jnp.concatenate([hot, hot], axis=1), asked)
         previous = prev_ref[t]
         truth = jnp.where(sub == lax.shift_right_logical(previous, 4), previous & 15, truth)
-    request_ref[...] = jnp.where(lane == 32, truth, request.astype(I32))
+    wide = jnp.concatenate([request.astype(I32), jnp.zeros((128, 96), I32)], axis=1)
+    request_ref[...] = jnp.where(lane == 32, truth, wide)
 
 
 def project_kernel(params_ref, out_ref, table_ref):
@@ -223,18 +221,24 @@
             )
             found_ref[32 * c + k : 32 * c + k + 1, :] = row[:, :128]
             found_ref[32 * c + k + 1 : 32 * c + k + 2, :] = row[:, 128:]
-    found_ref[288:, :] = jnp.zeros((96, 128), F32)
+    upper, middle, lower = split(found_ref[128:160, :], 3)
+    found_ref[320:352, :] = lower.astype(F32)
+    found_ref[352:, :] = jnp.zeros((32, 128), F32)
+    upper, lower = split(found_ref[256:288, :], 2)
+    found_ref[256:288, :] = upper.astype(F32)
+    found_ref[288:320, :] = lower.astype(F32)
     truth = jnp.dot(
         indicator(asked[:, 32:33] == iota((128, 16), 1)), image_ref[...],
         preferred_element_type=F32,
     )
+    spot = 0
     for i in range(3):
         block = found_ref[128 * i : 128 * (i + 1), :].T
-        for n, part in enumerate(split(block, 3)):
-            stage_ref[pl.ds(3 * i + n, 128, stride=16), :] = part.astype(F32)
+        for part in split(block, 3 - i):
+            stage_ref[pl.ds(spot, 128, stride=12), :] = part.astype(F32)
+            spot += 1
     for i in range(6):
-        stage_ref[pl.ds(9 + i, 128, stride=16), :] = truth[:, 128 * i : 128 * (i + 1)]
-    stage_ref[pl.ds(15, 128, stride=16), :] = jnp.zeros((128, 128), F32)
+        stage_ref[pl.ds(6 + i, 128, stride=12), :] = truth[:, 128 * i : 128 * (i + 1)]
     out_ref[...] = stage_ref[...].astype(BF16)
 
 
@@ -299,11 +303,15 @@
     code_ref[...] = (place_ref[...] >> 4) * 128 + holder_ref[...]
     low_ref[...] = place_ref[...] & 15
     stage_ref[...] = arrived_ref[...].astype(F32)
-    came = [stage_ref[pl.ds(i, 128, stride=16), :] for i in range(15)]
-    table = [(came[3 * i] + came[3 * i + 1] + came[3 * i + 2]).T for i in range(3)]
+    came = [stage_ref[pl.ds(i, 128, stride=12), :] for i in range(12)]
+    table = [(came[0] + came[1] + came[2]).T, (came[3] + came[4]).T, came[5].T]
     folded = []
     for c in range(9):
         part = table[c // 4][32 * (c % 4) : 32 * (c % 4) + 32, :]
+        if c == 4:
+            part = part + table[2][64:96, :]
+        if c == 8:
+            part = part + table[2][32:64, :]
         folded.append(jnp.concatenate([part[:16], part[16:]], axis=1))
     pieces = jnp.concatenate(split(jnp.concatenate(folded, axis=0), 3), axis=0)
     sub_slot = iota((256, 256), 0)
@@ -391,7 +399,7 @@
     chosen = indicator(source == iota((16, 128), 1))
     target = jnp.concatenate(
         [
-            jnp.dot(chosen, came[9 + i].astype(BF16), preferred_element_type=F32)
+            jnp.dot(chosen, came[6 + i].astype(BF16), preferred_element_type=F32)
             for i in range(6)
         ],
         axis=1,
@@ -669,10 +677,6 @@
     return lax.all_to_all(values, "dev", split_axis=0, concat_axis=0, tiled=True)
 
 
-def swap_rows(values, rows):
-    return swap(values.reshape(128, rows, 128)).reshape(128 * rows, 128)
-
-
 def body(
     params, entry_shard, entry_row, depth_order, live_count, tile_of_slot, prev_slot, gt_image
 ):
@@ -702,26 +706,26 @@
     )(params)
     picked = pl.pallas_call(
         pick_kernel,
-        out_shape=shape((2048, 128), BF16),
+        out_shape=shape((1536, 128), BF16),
         in_specs=[vmem(), vmem(), vmem()],
         out_specs=vmem(),
         scratch_shapes=[
             pltpu.VMEM((32, 128), I32),
             pltpu.VMEM((32, 128), I32),
             pltpu.VMEM((384, 128), F32),
-            pltpu.VMEM((2048, 128), F32),
+            pltpu.VMEM((1536, 128), F32),
         ],
         compiler_params=ROOM,
         name="pick",
     )(asked, table, gt_image)
-    arrived = swap_rows(picked, 16)
+    arrived = swap(picked.reshape(128, 3, 4, 128)).reshape(1536, 128)
     picture, loss, outgoing = pl.pallas_call(
         render_kernel,
         out_shape=(shape((16, 768)), shape((16, 128)), shape((384, 128))),
         in_specs=[vmem()] * 3 + [smem(), smem()],
         out_specs=(vmem(),) * 3,
         scratch_shapes=[
-            pltpu.VMEM((2048, 128), F32),
+            pltpu.VMEM((1536, 128), F32),
             pltpu.VMEM((256, 128), F32),
             pltpu.VMEM((2, 8, 128, 128), F32),
             pltpu.VMEM((2, 128, 128), F32),

time: 72.4 us -> 70.6 us (0.975)
  blocking collectives: 18 us -> 16.6 us
    all_to_all x1, blocking collectives: 18 us -> 16.6 us  [swap(): lax.all_to_all(values, 'dev', split_axis=0, concat_axis=0, tiled=True)]
where the time goes in v3:
time: 70.6 us; the launch traced here: 70.3 us
  Pallas kernels  17.8 us (25%)
  waiting for transfers between devices  16.8 us (24%)
  blocking collectives  16.6 us (24%)
  starting transfers between devices  16.1 us (23%)
  local copies, waits for them, and re-layouts  2.24 us (3%)
  between operations  0.71 us (1%)
    all_to_all x2, waiting for transfers between devices, swap(): lax.all_to_all(values, 'dev', split_axis=0, concat_axis=0, tiled=True)  16.8 us
    all_to_all x1, blocking collectives, swap(): lax.all_to_all(values, 'dev', split_axis=0, concat_axis=0, tiled=True)  16.6 us
    all_to_all x2, starting transfers between devices, swap(): lax.all_to_all(values, 'dev', split_axis=0, concat_axis=0, tiled=True)  16.1 us
    pallas_call x1, Pallas kernels, body(): pl.pallas_call(render_kernel, out_shape=(shape((16, 768)), shape((16, 128...  8.84 us
    pallas_call x1, Pallas kernels, body(): pl.pallas_call(update_kernel, out_shape=shape((59, 8192)), in_specs=[vmem...  3.61 us
    pallas_call x1, Pallas kernels, body(): pl.pallas_call(route_kernel, out_shape=(shape((128, 128), I32), shape((16...  2.42 us
    pallas_call x1, Pallas kernels, body(): pl.pallas_call(pick_kernel, out_shape=shape((1536, 128), BF16), in_specs=...  2.24 us
    unnamed x14, local copies, waits for them, and re-layouts  1.61 us
  transfers between devices with their start and end apart: 2, of which 2 were waited for; matrix products, arithmetic and copies ran while one was open for 1% of the time, Pallas kernels for 1%

profile of v3, /device:TPU:1, one launch (start us, length us, event | category | flops | bytes accessed | tf_op | source)
XLA Modules:
  0.0 70.3 jit_solution(4452548857799622514)
XLA Ops:
  0.6 0.0 copy-start.2
  0.6 2.4 %route.1 = (s32[128,128]{1,0:T(8,128)}, s32[16,128]{1,0:T(8,128)}, s32[16,128]{1,0:T(8,128)}) custom-call(s32[16,128]{1,0:T(8,128)} %shard_hbm.1, s32[16,128]{1,0:T(8,128)} %row_hbm.1, s32[16,128]{1,0:T(8,128)} %order_hbm.1, s32[16]{0:T(128)} %live_hbm.1, s32[16]{0:T(128)} %prev_ref.1), custom_call_target="tpu_custom_call" | custom-call | tf_op jit(solution)/shard_map/route/pallas_call | solution.py:683
  3.1 11.5 %all-to-all-start = ((s32[128,1,128]{2,1,0:T(1,128)}), s32[128,1,128]{2,1,0:T(1,128)S(1)}, u32[]{:S(2)}, u32[]{:S(2)}) async-start(s32[128,1,128]{2,1,0:T(1,128)} %bitcast.13), calls=%async_computation | async-start | bytes 131072 | tf_op jit(solution)/shard_map/all_to_all | solution.py:677
  14.6 0.0 copy-start
  14.6 1.6 %copy-done = f32[59,8192]{1,0:T(8,128)S(1)} copy-done((f32[59,8192]{1,0:T(8,128)S(1)}, f32[59,8192]{1,0:T(8,128)}, u32[]{:S(2)}) %copy-start) | copy-done | bytes 1933336
  16.2 0.0 copy-start.3
  16.2 0.0 copy-start.4
  16.2 0.0 copy-start.5
  16.2 0.0 copy-start.6
  16.2 0.0 copy-start.1
  16.2 0.7 %project.1.table_ref = bf16[864,256]{1,0:T(8,128)(2,1)S(1)} custom-call(f32[59,8192]{1,0:T(8,128)S(1)} %copy-done), custom_call_target="tpu_custom_call" | custom-call | flops 20000000 | bytes 20000000 | tf_op jit(solution)/shard_map/project/pallas_call | solution.py:695
  16.9 7.0 %all-to-all-done = s32[128,1,128]{2,1,0:T(1,128)S(1)} async-done(((s32[128,1,128]{2,1,0:T(1,128)}), s32[128,1,128]{2,1,0:T(1,128)S(1)}, u32[]{:S(2)}, u32[]{:S(2)}) %all-to-all-start) | async-done | bytes 65568 | tf_op jit(solution)/shard_map/all_to_all | solution.py:677
  23.9 0.0 copy-done.2
  23.9 2.2 %pick.1 = bf16[1536,128]{1,0:T(8,128)(2,1)S(1)} custom-call(s32[128,128]{1,0:T(8,128)S(1)} %bitcast.11, bf16[864,256]{1,0:T(8,128)(2,1)S(1)} %project.1.table_ref, bf16[16,768]{1,0:T(8,128)(2,1)S(1)} %copy-done.2), custom_call_target="tpu_custom_call" | custom-call | tf_op jit(solution)/shard_map/pick/pallas_call | solution.py:707
  26.2 16.6 %all_to_all.21 = bf16[128,3,4,128]{3,2,1,0:T(4,128)(2,1)S(1)} all-to-all(bf16[128,3,4,128]{3,2,1,0:T(4,128)(2,1)S(1)} %bitcast.9), channel_id=1, replica_groups=mesh['dev'=128] {'dev'}, dimensions={0} | all-to-all | bytes 786432 | tf_op jit(solution)/shard_map/all_to_all | solution.py:677
  42.8 0.0 copy-done.3
  42.8 0.0 copy-done.4
  42.8 0.0 copy-done.5
  42.8 0.0 copy-done.6
  42.8 8.8 %render.1 = (f32[16,768]{1,0:T(8,128)}, f32[16,128]{1,0:T(8,128)S(1)}, f32[384,128]{1,0:T(8,128)}) custom-call(bf16[1536,128]{1,0:T(8,128)(2,1)S(1)} %bitcast.8, s32[16,128]{1,0:T(8,128)S(1)} %copy-done.3, s32[16,128]{1,0:T(8,128)S(1)} %copy-done.4, s32[16]{0:T(128)S(1)} %copy-done.6, s32[16]{0:T(128)S(1)} %copy-done.5), custom_call_target="tpu_custom_call" | custom-call | tf_op jit(solution)/shard_map/render/pallas_call | solution.py:722
  51.6 4.6 %all-to-all-start.2 = ((f32[128,1,384]{2,1,0:T(1,128)}), f32[128,1,384]{2,1,0:T(1,128)S(1)}, u32[]{:S(2)}, u32[]{:S(2)}) async-start(f32[128,1,384]{2,1,0:T(1,128)} %bitcast.5), calls=%async_computation.2 | async-start | bytes 393216 | tf_op jit(solution)/shard_map/all_to_all | solution.py:677
  56.2 0.6 slice_reduce_fusion
  56.9 9.9 %all-to-all-done.2 = f32[128,1,384]{2,1,0:T(1,128)S(1)} async-done(((f32[128,1,384]{2,1,0:T(1,128)}), f32[128,1,384]{2,1,0:T(1,128)S(1)}, u32[]{:S(2)}, u32[]{:S(2)}) %all-to-all-start.2) | async-done | bytes 196640 | tf_op jit(solution)/shard_map/all_to_all | solution.py:677
  66.7 0.0 copy-done.1
  66.7 3.6 %update.1 = f32[59,8192]{1,0:T(8,128)} custom-call(f32[384,128]{1,0:T(8,128)S(1)} %bitcast.10, s32[128,128]{1,0:T(8,128)S(1)} %bitcast.12, f32[59,8192]{1,0:T(8,128)S(1)} %copy-done.1), custom_call_target="tpu_custom_call" | custom-call | tf_op jit(solution)/shard_map/update/pallas_call | solution.py:745
Async XLA Ops:
  0.6 23.3 %copy-start.2 = (bf16[16,768]{1,0:T(8,128)(2,1)S(1)}, bf16[16,768]{1,0:T(8,128)(2,1)}, u32[]{:S(2)}) copy-start(bf16[16,768]{1,0:T(8,128)(2,1)} %image_ref.1) | copy-start | bytes 73732
  3.1 20.8 %all-to-all-start = ((s32[128,1,128]{2,1,0:T(1,128)}), s32[128,1,128]{2,1,0:T(1,128)S(1)}, u32[]{:S(2)}, u32[]{:S(2)}) async-start(s32[128,1,128]{2,1,0:T(1,128)} %bitcast.13), calls=%async_computation | async-start | bytes 131072 | tf_op jit(solution)/shard_map/all_to_all | solution.py:677
  14.6 1.6 %copy-start = (f32[59,8192]{1,0:T(8,128)S(1)}, f32[59,8192]{1,0:T(8,128)}, u32[]{:S(2)}) copy-start(f32[59,8192]{1,0:T(8,128)} %params_ref.3) | copy-start | bytes 5799940
  16.2 26.6 %copy-start.3 = (s32[16,128]{1,0:T(8,128)S(1)}, s32[16,128]{1,0:T(8,128)}, u32[]{:S(2)}) copy-start(s32[16,128]{1,0:T(8,128)} %get-tuple-element.10.holder_ref) | copy-start | bytes 24580
  16.2 26.6 %copy-start.4 = (s32[16,128]{1,0:T(8,128)S(1)}, s32[16,128]{1,0:T(8,128)}, u32[]{:S(2)}) copy-start(s32[16,128]{1,0:T(8,128)} %get-tuple-element.11.place_ref) | copy-start | bytes 24580
  16.2 26.6 %copy-start.5 = (s32[16]{0:T(128)S(1)}, s32[16]{0:T(128)}, u32[]{:S(2)}) copy-start(s32[16]{0:T(128)} %prev_ref.1) | copy-start | bytes 196
  16.2 26.6 %copy-start.6 = (s32[16]{0:T(128)S(1)}, s32[16]{0:T(128)}, u32[]{:S(2)}) copy-start(s32[16]{0:T(128)} %tile_ref.1) | copy-start | bytes 196
  16.2 50.5 %copy-start.1 = (f32[59,8192]{1,0:T(8,128)S(1)}, f32[59,8192]{1,0:T(8,128)}, u32[]{:S(2)}) copy-start(f32[59,8192]{1,0:T(8,128)} %params_ref.3) | copy-start | bytes 5799940
  51.6 15.1 %all-to-all-start.2 = ((f32[128,1,384]{2,1,0:T(1,128)}), f32[128,1,384]{2,1,0:T(1,128)S(1)}, u32[]{:S(2)}, u32[]{:S(2)}) async-start(f32[128,1,384]{2,1,0:T(1,128)} %bitcast.5), calls=%async_computation.2 | async-start | bytes 393216 | tf_op jit(solution)/shard_map/all_to_all | solution.py:677

commit v4 on v3

--- a/solution.py
+++ b/solution.py
@@ -197,8 +197,10 @@
 
     for half in range(2):
         lax.fori_loop(0, 4, lambda b, unused, half=half: (step(b, half), unused)[1], 0)
-    for n, part in enumerate(split(table_ref[...], 3)):
-        out_ref[288 * n : 288 * (n + 1), :] = part
+    upper, middle, lower = split(table_ref[...], 3)
+    out_ref[0:288, :] = upper
+    out_ref[288:576, :] = middle
+    out_ref[576:736, :] = lower[:160]
 
 
 def pick_kernel(
@@ -213,7 +215,8 @@
     for k in range(0, 32, 2):
         hot = indicator(pair_rows(low_ref, k, 256) == sub_low)
         parts = jnp.dot(table_ref[...], hot, preferred_element_type=F32)
-        whole = parts[:288] + parts[288:576] + parts[576:]
+        both = parts[:288] + parts[288:576]
+        whole = jnp.concatenate([both[:160] + parts[576:], both[160:]], axis=0)
         match = pair_rows(high_ref, k, 32) == sub_high
         for c in range(9):
             row = jnp.sum(
@@ -694,7 +697,7 @@
     asked = swap(request)
     table = pl.pallas_call(
         project_kernel,
-        out_shape=shape((864, 256), BF16),
+        out_shape=shape((736, 256), BF16),
         in_specs=[vmem()],
         out_specs=vmem(),
         scratch_shapes=[pltpu.VMEM((288, 256), F32)],

time: 70.6 us -> 70.3 us (level)
  no operation moved by 1% of the time
where the time goes in v4:
time: 70.3 us; the launch traced here: 70.1 us
  Pallas kernels  17.5 us (25%)
  waiting for transfers between devices  16.9 us (24%)
  blocking collectives  16.6 us (24%)
  starting transfers between devices  16.1 us (23%)
  local copies, waits for them, and re-layouts  2.24 us (3%)
  between operations  0.72 us (1%)
    all_to_all x2, waiting for transfers between devices, swap(): lax.all_to_all(values, 'dev', split_axis=0, concat_axis=0, tiled=True)  16.9 us
    all_to_all x1, blocking collectives, swap(): lax.all_to_all(values, 'dev', split_axis=0, concat_axis=0, tiled=True)  16.6 us
    all_to_all x2, starting transfers between devices, swap(): lax.all_to_all(values, 'dev', split_axis=0, concat_axis=0, tiled=True)  16.1 us
    pallas_call x1, Pallas kernels, body(): pl.pallas_call(render_kernel, out_shape=(shape((16, 768)), shape((16, 128...  8.84 us
    pallas_call x1, Pallas kernels, body(): pl.pallas_call(update_kernel, out_shape=shape((59, 8192)), in_specs=[vmem...  3.61 us
    pallas_call x1, Pallas kernels, body(): pl.pallas_call(route_kernel, out_shape=(shape((128, 128), I32), shape((16...  2.42 us
    pallas_call x1, Pallas kernels, body(): pl.pallas_call(pick_kernel, out_shape=shape((1536, 128), BF16), in_specs=...  1.96 us
    unnamed x14, local copies, waits for them, and re-layouts  1.61 us
  transfers between devices with their start and end apart: 2, of which 2 were waited for; matrix products, arithmetic and copies ran while one was open for 1% of the time, Pallas kernels for 1%

profile of v4, /device:TPU:1, one launch (start us, length us, event | category | flops | bytes accessed | tf_op | source)
XLA Modules:
  0.0 70.1 jit_solution(1459853099420257363)
XLA Ops:
  0.6 0.0 copy-start.2
  0.6 2.4 %route.1 = (s32[128,128]{1,0:T(8,128)}, s32[16,128]{1,0:T(8,128)}, s32[16,128]{1,0:T(8,128)}) custom-call(s32[16,128]{1,0:T(8,128)} %shard_hbm.1, s32[16,128]{1,0:T(8,128)} %row_hbm.1, s32[16,128]{1,0:T(8,128)} %order_hbm.1, s32[16]{0:T(128)} %live_hbm.1, s32[16]{0:T(128)} %prev_ref.1), custom_call_target="tpu_custom_call" | custom-call | tf_op jit(solution)/shard_map/route/pallas_call | solution.py:686
  3.1 11.5 %all-to-all-start = ((s32[128,1,128]{2,1,0:T(1,128)}), s32[128,1,128]{2,1,0:T(1,128)S(1)}, u32[]{:S(2)}, u32[]{:S(2)}) async-start(s32[128,1,128]{2,1,0:T(1,128)} %bitcast.13), calls=%async_computation | async-start | bytes 131072 | tf_op jit(solution)/shard_map/all_to_all | solution.py:680
  14.6 0.0 copy-start
  14.6 1.6 %copy-done = f32[59,8192]{1,0:T(8,128)S(1)} copy-done((f32[59,8192]{1,0:T(8,128)S(1)}, f32[59,8192]{1,0:T(8,128)}, u32[]{:S(2)}) %copy-start) | copy-done | bytes 1933336
  16.2 0.0 copy-start.3
  16.2 0.0 copy-start.4
  16.2 0.0 copy-start.5
  16.2 0.0 copy-start.6
  16.2 0.0 copy-start.1
  16.2 0.7 %project.1.table_ref = bf16[736,256]{1,0:T(8,128)(2,1)S(1)} custom-call(f32[59,8192]{1,0:T(8,128)S(1)} %copy-done), custom_call_target="tpu_custom_call" | custom-call | flops 20000000 | bytes 20000000 | tf_op jit(solution)/shard_map/project/pallas_call | solution.py:698
  16.9 7.0 %all-to-all-done = s32[128,1,128]{2,1,0:T(1,128)S(1)} async-done(((s32[128,1,128]{2,1,0:T(1,128)}), s32[128,1,128]{2,1,0:T(1,128)S(1)}, u32[]{:S(2)}, u32[]{:S(2)}) %all-to-all-start) | async-done | bytes 65568 | tf_op jit(solution)/shard_map/all_to_all | solution.py:680
  23.9 0.0 copy-done.2
  23.9 2.0 %pick.1 = bf16[1536,128]{1,0:T(8,128)(2,1)S(1)} custom-call(s32[128,128]{1,0:T(8,128)S(1)} %bitcast.11, bf16[736,256]{1,0:T(8,128)(2,1)S(1)} %project.1.table_ref, bf16[16,768]{1,0:T(8,128)(2,1)S(1)} %copy-done.2), custom_call_target="tpu_custom_call" | custom-call | tf_op jit(solution)/shard_map/pick/pallas_call | solution.py:710
  25.9 16.6 %all_to_all.21 = bf16[128,3,4,128]{3,2,1,0:T(4,128)(2,1)S(1)} all-to-all(bf16[128,3,4,128]{3,2,1,0:T(4,128)(2,1)S(1)} %bitcast.9), channel_id=1, replica_groups=mesh['dev'=128] {'dev'}, dimensions={0} | all-to-all | bytes 786432 | tf_op jit(solution)/shard_map/all_to_all | solution.py:680
  42.5 0.0 copy-done.3
  42.5 0.0 copy-done.4
  42.5 0.0 copy-done.5
  42.5 0.0 copy-done.6
  42.5 8.8 %render.1 = (f32[16,768]{1,0:T(8,128)}, f32[16,128]{1,0:T(8,128)S(1)}, f32[384,128]{1,0:T(8,128)}) custom-call(bf16[1536,128]{1,0:T(8,128)(2,1)S(1)} %bitcast.8, s32[16,128]{1,0:T(8,128)S(1)} %copy-done.3, s32[16,128]{1,0:T(8,128)S(1)} %copy-done.4, s32[16]{0:T(128)S(1)} %copy-done.6, s32[16]{0:T(128)S(1)} %copy-done.5), custom_call_target="tpu_custom_call" | custom-call | tf_op jit(solution)/shard_map/render/pallas_call | solution.py:725
  51.4 4.6 %all-to-all-start.2 = ((f32[128,1,384]{2,1,0:T(1,128)}), f32[128,1,384]{2,1,0:T(1,128)S(1)}, u32[]{:S(2)}, u32[]{:S(2)}) async-start(f32[128,1,384]{2,1,0:T(1,128)} %bitcast.5), calls=%async_computation.2 | async-start | bytes 393216 | tf_op jit(solution)/shard_map/all_to_all | solution.py:680
  56.0 0.6 slice_reduce_fusion
  56.6 9.9 %all-to-all-done.2 = f32[128,1,384]{2,1,0:T(1,128)S(1)} async-done(((f32[128,1,384]{2,1,0:T(1,128)}), f32[128,1,384]{2,1,0:T(1,128)S(1)}, u32[]{:S(2)}, u32[]{:S(2)}) %all-to-all-start.2) | async-done | bytes 196640 | tf_op jit(solution)/shard_map/all_to_all | solution.py:680
  66.4 0.0 copy-done.1
  66.4 3.6 %update.1 = f32[59,8192]{1,0:T(8,128)} custom-call(f32[384,128]{1,0:T(8,128)S(1)} %bitcast.10, s32[128,128]{1,0:T(8,128)S(1)} %bitcast.12, f32[59,8192]{1,0:T(8,128)S(1)} %copy-done.1), custom_call_target="tpu_custom_call" | custom-call | tf_op jit(solution)/shard_map/update/pallas_call | solution.py:748
Async XLA Ops:
  0.6 23.3 %copy-start.2 = (bf16[16,768]{1,0:T(8,128)(2,1)S(1)}, bf16[16,768]{1,0:T(8,128)(2,1)}, u32[]{:S(2)}) copy-start(bf16[16,768]{1,0:T(8,128)(2,1)} %image_ref.1) | copy-start | bytes 73732
  3.1 20.8 %all-to-all-start = ((s32[128,1,128]{2,1,0:T(1,128)}), s32[128,1,128]{2,1,0:T(1,128)S(1)}, u32[]{:S(2)}, u32[]{:S(2)}) async-start(s32[128,1,128]{2,1,0:T(1,128)} %bitcast.13), calls=%async_computation | async-start | bytes 131072 | tf_op jit(solution)/shard_map/all_to_all | solution.py:680
  14.6 1.6 %copy-start = (f32[59,8192]{1,0:T(8,128)S(1)}, f32[59,8192]{1,0:T(8,128)}, u32[]{:S(2)}) copy-start(f32[59,8192]{1,0:T(8,128)} %params_ref.3) | copy-start | bytes 5799940
  16.2 26.3 %copy-start.3 = (s32[16,128]{1,0:T(8,128)S(1)}, s32[16,128]{1,0:T(8,128)}, u32[]{:S(2)}) copy-start(s32[16,128]{1,0:T(8,128)} %get-tuple-element.10.holder_ref) | copy-start | bytes 24580
  16.2 26.3 %copy-start.4 = (s32[16,128]{1,0:T(8,128)S(1)}, s32[16,128]{1,0:T(8,128)}, u32[]{:S(2)}) copy-start(s32[16,128]{1,0:T(8,128)} %get-tuple-element.11.place_ref) | copy-start | bytes 24580
  16.2 26.3 %copy-start.5 = (s32[16]{0:T(128)S(1)}, s32[16]{0:T(128)}, u32[]{:S(2)}) copy-start(s32[16]{0:T(128)} %prev_ref.1) | copy-start | bytes 196
  16.2 26.3 %copy-start.6 = (s32[16]{0:T(128)S(1)}, s32[16]{0:T(128)}, u32[]{:S(2)}) copy-start(s32[16]{0:T(128)} %tile_ref.1) | copy-start | bytes 196
  16.2 50.3 %copy-start.1 = (f32[59,8192]{1,0:T(8,128)S(1)}, f32[59,8192]{1,0:T(8,128)}, u32[]{:S(2)}) copy-start(f32[59,8192]{1,0:T(8,128)} %params_ref.3) | copy-start | bytes 5799940
  51.4 15.1 %all-to-all-start.2 = ((f32[128,1,384]{2,1,0:T(1,128)}), f32[128,1,384]{2,1,0:T(1,128)S(1)}, u32[]{:S(2)}, u32[]{:S(2)}) async-start(f32[128,1,384]{2,1,0:T(1,128)} %bitcast.5), calls=%async_computation.2 | async-start | bytes 393216 | tf_op jit(solution)/shard_map/all_to_all | solution.py:680

commit v5 on v4

--- a/solution.py
+++ b/solution.py
@@ -299,7 +299,7 @@
 
 def render_kernel(
     arrived_ref, holder_ref, place_ref, tile_ref, prev_ref,
-    picture_ref, loss_ref, out_ref, stage_ref,
+    picture_hbm, loss_ref, out_ref, picture_ref, picture_sem, stage_ref,
     ordered_ref, row_ref, dx_ref, alpha_ref, weight_ref, reach_ref, moment_ref, found_ref,
     code_ref, low_ref, part_ref,
 ):
@@ -420,6 +420,8 @@
         )
         picture_ref[:, 256 * k : 256 * (k + 1)] = image
         images.append(image)
+    picture_copy = pltpu.make_async_copy(picture_ref, picture_hbm, picture_sem)
+    picture_copy.start()
     loss, slopes = loss_and_slopes(images, target)
     loss_ref[...] = jnp.broadcast_to(loss, (16, 128))
     slope = [
@@ -550,6 +552,7 @@
     found_ref[0:288, :] = total
     found_ref[288:, :] = jnp.zeros((96, 128), F32)
     put_rows(out_ref, found_ref)
+    picture_copy.wait()
 
 
 def update_kernel(
@@ -647,7 +650,7 @@
         leave(block).start()
 
     for half in range(2):
-        lax.fori_loop(0, 4, lambda b, unused, half=half: (pull(b, half), unused)[1], 0)
+        lax.fori_loop(0, 4, lambda b, unused, half=half: (pull(b, half), unused)[1], 0, unroll=2)
     for block in range(8):
         leave(block).wait()
 
@@ -726,8 +729,10 @@
         render_kernel,
         out_shape=(shape((16, 768)), shape((16, 128)), shape((384, 128))),
         in_specs=[vmem()] * 3 + [smem(), smem()],
-        out_specs=(vmem(),) * 3,
+        out_specs=(anywhere(), vmem(), vmem()),
         scratch_shapes=[
+            pltpu.VMEM((16, 768), F32),
+            pltpu.SemaphoreType.DMA,
             pltpu.VMEM((1536, 128), F32),
             pltpu.VMEM((256, 128), F32),
             pltpu.VMEM((2, 8, 128, 128), F32),

time: 70.3 us -> 70.4 us (level)
  no operation moved by 1% of the time
where the time goes in v5:
time: 70.4 us; the launch traced here: 70.1 us
  Pallas kernels  17.6 us (25%)
  waiting for transfers between devices  16.9 us (24%)
  blocking collectives  16.6 us (24%)
  starting transfers between devices  16.1 us (23%)
  local copies, waits for them, and re-layouts  2.24 us (3%)
  between operations  0.72 us (1%)
    all_to_all x2, waiting for transfers between devices, swap(): lax.all_to_all(values, 'dev', split_axis=0, concat_axis=0, tiled=True)  16.9 us
    all_to_all x1, blocking collectives, swap(): lax.all_to_all(values, 'dev', split_axis=0, concat_axis=0, tiled=True)  16.6 us
    all_to_all x2, starting transfers between devices, swap(): lax.all_to_all(values, 'dev', split_axis=0, concat_axis=0, tiled=True)  16.1 us
    pallas_call x1, Pallas kernels, body(): pl.pallas_call(render_kernel, out_shape=(shape((16, 768)), shape((16, 128...  8.84 us
    pallas_call x1, Pallas kernels, body(): pl.pallas_call(update_kernel, out_shape=shape((59, 8192)), in_specs=[vmem...  3.66 us
    pallas_call x1, Pallas kernels, body(): pl.pallas_call(route_kernel, out_shape=(shape((128, 128), I32), shape((16...  2.42 us
    pallas_call x1, Pallas kernels, body(): pl.pallas_call(pick_kernel, out_shape=shape((1536, 128), BF16), in_specs=...  1.96 us
    unnamed x14, local copies, waits for them, and re-layouts  1.61 us
  transfers between devices with their start and end apart: 2, of which 2 were waited for; matrix products, arithmetic and copies ran while one was open for 1% of the time, Pallas kernels for 1%

profile of v5, /device:TPU:1, one launch (start us, length us, event | category | flops | bytes accessed | tf_op | source)
XLA Modules:
  0.0 70.1 jit_solution(6830144118661252287)
XLA Ops:
  0.6 0.0 copy-start.2
  0.6 2.4 %route.1 = (s32[128,128]{1,0:T(8,128)}, s32[16,128]{1,0:T(8,128)}, s32[16,128]{1,0:T(8,128)}) custom-call(s32[16,128]{1,0:T(8,128)} %shard_hbm.1, s32[16,128]{1,0:T(8,128)} %row_hbm.1, s32[16,128]{1,0:T(8,128)} %order_hbm.1, s32[16]{0:T(128)} %live_hbm.1, s32[16]{0:T(128)} %prev_ref.1), custom_call_target="tpu_custom_call" | custom-call | tf_op jit(solution)/shard_map/route/pallas_call | solution.py:689
  3.1 11.5 %all-to-all-start = ((s32[128,1,128]{2,1,0:T(1,128)}), s32[128,1,128]{2,1,0:T(1,128)S(1)}, u32[]{:S(2)}, u32[]{:S(2)}) async-start(s32[128,1,128]{2,1,0:T(1,128)} %bitcast.13), calls=%async_computation | async-start | bytes 131072 | tf_op jit(solution)/shard_map/all_to_all | solution.py:683
  14.6 0.0 copy-start
  14.6 1.6 %copy-done = f32[59,8192]{1,0:T(8,128)S(1)} copy-done((f32[59,8192]{1,0:T(8,128)S(1)}, f32[59,8192]{1,0:T(8,128)}, u32[]{:S(2)}) %copy-start) | copy-done | bytes 1933336
  16.2 0.0 copy-start.3
  16.2 0.0 copy-start.4
  16.2 0.0 copy-start.5
  16.2 0.0 copy-start.6
  16.2 0.0 copy-start.1
  16.2 0.7 %project.1.table_ref = bf16[736,256]{1,0:T(8,128)(2,1)S(1)} custom-call(f32[59,8192]{1,0:T(8,128)S(1)} %copy-done), custom_call_target="tpu_custom_call" | custom-call | flops 20000000 | bytes 20000000 | tf_op jit(solution)/shard_map/project/pallas_call | solution.py:701
  16.9 7.0 %all-to-all-done = s32[128,1,128]{2,1,0:T(1,128)S(1)} async-done(((s32[128,1,128]{2,1,0:T(1,128)}), s32[128,1,128]{2,1,0:T(1,128)S(1)}, u32[]{:S(2)}, u32[]{:S(2)}) %all-to-all-start) | async-done | bytes 65568 | tf_op jit(solution)/shard_map/all_to_all | solution.py:683
  23.9 0.0 copy-done.2
  23.9 2.0 %pick.1 = bf16[1536,128]{1,0:T(8,128)(2,1)S(1)} custom-call(s32[128,128]{1,0:T(8,128)S(1)} %bitcast.11, bf16[736,256]{1,0:T(8,128)(2,1)S(1)} %project.1.table_ref, bf16[16,768]{1,0:T(8,128)(2,1)S(1)} %copy-done.2), custom_call_target="tpu_custom_call" | custom-call | tf_op jit(solution)/shard_map/pick/pallas_call | solution.py:713
  25.9 16.6 %all_to_all.21 = bf16[128,3,4,128]{3,2,1,0:T(4,128)(2,1)S(1)} all-to-all(bf16[128,3,4,128]{3,2,1,0:T(4,128)(2,1)S(1)} %bitcast.9), channel_id=1, replica_groups=mesh['dev'=128] {'dev'}, dimensions={0} | all-to-all | bytes 786432 | tf_op jit(solution)/shard_map/all_to_all | solution.py:683
  42.5 0.0 copy-done.3
  42.5 0.0 copy-done.4
  42.5 0.0 copy-done.5
  42.5 0.0 copy-done.6
  42.5 8.8 %render.1 = (f32[16,768]{1,0:T(8,128)}, f32[16,128]{1,0:T(8,128)S(1)}, f32[384,128]{1,0:T(8,128)}) custom-call(bf16[1536,128]{1,0:T(8,128)(2,1)S(1)} %bitcast.8, s32[16,128]{1,0:T(8,128)S(1)} %copy-done.3, s32[16,128]{1,0:T(8,128)S(1)} %copy-done.4, s32[16]{0:T(128)S(1)} %copy-done.6, s32[16]{0:T(128)S(1)} %copy-done.5), custom_call_target="tpu_custom_call" | custom-call | tf_op jit(solution)/shard_map/render/pallas_call | solution.py:728
  51.4 4.6 %all-to-all-start.2 = ((f32[128,1,384]{2,1,0:T(1,128)}), f32[128,1,384]{2,1,0:T(1,128)S(1)}, u32[]{:S(2)}, u32[]{:S(2)}) async-start(f32[128,1,384]{2,1,0:T(1,128)} %bitcast.5), calls=%async_computation.2 | async-start | bytes 393216 | tf_op jit(solution)/shard_map/all_to_all | solution.py:683
  56.0 0.6 slice_reduce_fusion
  56.6 9.9 %all-to-all-done.2 = f32[128,1,384]{2,1,0:T(1,128)S(1)} async-done(((f32[128,1,384]{2,1,0:T(1,128)}), f32[128,1,384]{2,1,0:T(1,128)S(1)}, u32[]{:S(2)}, u32[]{:S(2)}) %all-to-all-start.2) | async-done | bytes 196640 | tf_op jit(solution)/shard_map/all_to_all | solution.py:683
  66.5 0.0 copy-done.1
  66.5 3.7 %update.1 = f32[59,8192]{1,0:T(8,128)} custom-call(f32[384,128]{1,0:T(8,128)S(1)} %bitcast.10, s32[128,128]{1,0:T(8,128)S(1)} %bitcast.12, f32[59,8192]{1,0:T(8,128)S(1)} %copy-done.1), custom_call_target="tpu_custom_call" | custom-call | tf_op jit(solution)/shard_map/update/pallas_call | solution.py:753
Async XLA Ops:
  0.6 23.3 %copy-start.2 = (bf16[16,768]{1,0:T(8,128)(2,1)S(1)}, bf16[16,768]{1,0:T(8,128)(2,1)}, u32[]{:S(2)}) copy-start(bf16[16,768]{1,0:T(8,128)(2,1)} %image_ref.1) | copy-start | bytes 73732
  3.1 20.8 %all-to-all-start = ((s32[128,1,128]{2,1,0:T(1,128)}), s32[128,1,128]{2,1,0:T(1,128)S(1)}, u32[]{:S(2)}, u32[]{:S(2)}) async-start(s32[128,1,128]{2,1,0:T(1,128)} %bitcast.13), calls=%async_computation | async-start | bytes 131072 | tf_op jit(solution)/shard_map/all_to_all | solution.py:683
  14.6 1.6 %copy-start = (f32[59,8192]{1,0:T(8,128)S(1)}, f32[59,8192]{1,0:T(8,128)}, u32[]{:S(2)}) copy-start(f32[59,8192]{1,0:T(8,128)} %params_ref.3) | copy-start | bytes 5799940
  16.2 26.3 %copy-start.3 = (s32[16,128]{1,0:T(8,128)S(1)}, s32[16,128]{1,0:T(8,128)}, u32[]{:S(2)}) copy-start(s32[16,128]{1,0:T(8,128)} %get-tuple-element.10.holder_ref) | copy-start | bytes 24580
  16.2 26.3 %copy-start.4 = (s32[16,128]{1,0:T(8,128)S(1)}, s32[16,128]{1,0:T(8,128)}, u32[]{:S(2)}) copy-start(s32[16,128]{1,0:T(8,128)} %get-tuple-element.11.place_ref) | copy-start | bytes 24580
  16.2 26.3 %copy-start.5 = (s32[16]{0:T(128)S(1)}, s32[16]{0:T(128)}, u32[]{:S(2)}) copy-start(s32[16]{0:T(128)} %prev_ref.1) | copy-start | bytes 196
  16.2 26.3 %copy-start.6 = (s32[16]{0:T(128)S(1)}, s32[16]{0:T(128)}, u32[]{:S(2)}) copy-start(s32[16]{0:T(128)} %tile_ref.1) | copy-start | bytes 196
  16.2 50.3 %copy-start.1 = (f32[59,8192]{1,0:T(8,128)S(1)}, f32[59,8192]{1,0:T(8,128)}, u32[]{:S(2)}) copy-start(f32[59,8192]{1,0:T(8,128)} %params_ref.3) | copy-start | bytes 5799940
  51.4 15.1 %all-to-all-start.2 = ((f32[128,1,384]{2,1,0:T(1,128)}), f32[128,1,384]{2,1,0:T(1,128)S(1)}, u32[]{:S(2)}, u32[]{:S(2)}) async-start(f32[128,1,384]{2,1,0:T(1,128)} %bitcast.5), calls=%async_computation.2 | async-start | bytes 393216 | tf_op jit(solution)/shard_map/all_to_all | solution.py:683

commit v6 on v5

--- a/solution.py
+++ b/solution.py
@@ -672,7 +672,7 @@
 
 
 PICK_UNROLL = 4
-FORWARD_UNROLL = 4
+FORWARD_UNROLL = 8
 SCATTER_UNROLL = 16
 GIVE_UNROLL = 4
 WIDE = pltpu.CompilerParams(vmem_limit_bytes=58 * 1024 * 1024)

time: 70.4 us -> 70.2 us (level)
  no operation moved by 1% of the time
where the time goes in v6:
time: 70.2 us; the launch traced here: 69.9 us
  Pallas kernels  17.4 us (25%)
  waiting for transfers between devices  16.9 us (24%)
  blocking collectives  16.6 us (24%)
  starting transfers between devices  16.1 us (23%)
  local copies, waits for them, and re-layouts  2.24 us (3%)
  between operations  0.72 us (1%)
    all_to_all x2, waiting for transfers between devices, swap(): lax.all_to_all(values, 'dev', split_axis=0, concat_axis=0, tiled=True)  16.9 us
    all_to_all x1, blocking collectives, swap(): lax.all_to_all(values, 'dev', split_axis=0, concat_axis=0, tiled=True)  16.6 us
    all_to_all x2, starting transfers between devices, swap(): lax.all_to_all(values, 'dev', split_axis=0, concat_axis=0, tiled=True)  16.1 us
    pallas_call x1, Pallas kernels, body(): pl.pallas_call(render_kernel, out_shape=(shape((16, 768)), shape((16, 128...  8.62 us
    pallas_call x1, Pallas kernels, body(): pl.pallas_call(update_kernel, out_shape=shape((59, 8192)), in_specs=[vmem...  3.66 us
    pallas_call x1, Pallas kernels, body(): pl.pallas_call(route_kernel, out_shape=(shape((128, 128), I32), shape((16...  2.42 us
    pallas_call x1, Pallas kernels, body(): pl.pallas_call(pick_kernel, out_shape=shape((1536, 128), BF16), in_specs=...  1.96 us
    unnamed x14, local copies, waits for them, and re-layouts  1.61 us
  transfers between devices with their start and end apart: 2, of which 2 were waited for; matrix products, arithmetic and copies ran while one was open for 1% of the time, Pallas kernels for 1%

profile of v6, /device:TPU:1, one launch (start us, length us, event | category | flops | bytes accessed | tf_op | source)
XLA Modules:
  0.0 69.9 jit_solution(12942968763517015798)
XLA Ops:
  0.6 0.0 copy-start.2
  0.6 2.4 %route.1 = (s32[128,128]{1,0:T(8,128)}, s32[16,128]{1,0:T(8,128)}, s32[16,128]{1,0:T(8,128)}) custom-call(s32[16,128]{1,0:T(8,128)} %shard_hbm.1, s32[16,128]{1,0:T(8,128)} %row_hbm.1, s32[16,128]{1,0:T(8,128)} %order_hbm.1, s32[16]{0:T(128)} %live_hbm.1, s32[16]{0:T(128)} %prev_ref.1), custom_call_target="tpu_custom_call" | custom-call | tf_op jit(solution)/shard_map/route/pallas_call | solution.py:689
  3.1 11.5 %all-to-all-start = ((s32[128,1,128]{2,1,0:T(1,128)}), s32[128,1,128]{2,1,0:T(1,128)S(1)}, u32[]{:S(2)}, u32[]{:S(2)}) async-start(s32[128,1,128]{2,1,0:T(1,128)} %bitcast.13), calls=%async_computation | async-start | bytes 131072 | tf_op jit(solution)/shard_map/all_to_all | solution.py:683
  14.6 0.0 copy-start
  14.6 1.6 %copy-done = f32[59,8192]{1,0:T(8,128)S(1)} copy-done((f32[59,8192]{1,0:T(8,128)S(1)}, f32[59,8192]{1,0:T(8,128)}, u32[]{:S(2)}) %copy-start) | copy-done | bytes 1933336
  16.2 0.0 copy-start.3
  16.2 0.0 copy-start.4
  16.2 0.0 copy-start.5
  16.2 0.0 copy-start.6
  16.2 0.0 copy-start.1
  16.2 0.7 %project.1.table_ref = bf16[736,256]{1,0:T(8,128)(2,1)S(1)} custom-call(f32[59,8192]{1,0:T(8,128)S(1)} %copy-done), custom_call_target="tpu_custom_call" | custom-call | flops 20000000 | bytes 20000000 | tf_op jit(solution)/shard_map/project/pallas_call | solution.py:701
  16.9 7.0 %all-to-all-done = s32[128,1,128]{2,1,0:T(1,128)S(1)} async-done(((s32[128,1,128]{2,1,0:T(1,128)}), s32[128,1,128]{2,1,0:T(1,128)S(1)}, u32[]{:S(2)}, u32[]{:S(2)}) %all-to-all-start) | async-done | bytes 65568 | tf_op jit(solution)/shard_map/all_to_all | solution.py:683
  23.9 0.0 copy-done.2
  23.9 2.0 %pick.1 = bf16[1536,128]{1,0:T(8,128)(2,1)S(1)} custom-call(s32[128,128]{1,0:T(8,128)S(1)} %bitcast.11, bf16[736,256]{1,0:T(8,128)(2,1)S(1)} %project.1.table_ref, bf16[16,768]{1,0:T(8,128)(2,1)S(1)} %copy-done.2), custom_call_target="tpu_custom_call" | custom-call | tf_op jit(solution)/shard_map/pick/pallas_call | solution.py:713
  25.9 16.6 %all_to_all.21 = bf16[128,3,4,128]{3,2,1,0:T(4,128)(2,1)S(1)} all-to-all(bf16[128,3,4,128]{3,2,1,0:T(4,128)(2,1)S(1)} %bitcast.9), channel_id=1, replica_groups=mesh['dev'=128] {'dev'}, dimensions={0} | all-to-all | bytes 786432 | tf_op jit(solution)/shard_map/all_to_all | solution.py:683
  42.5 0.0 copy-done.3
  42.5 0.0 copy-done.4
  42.5 0.0 copy-done.5
  42.5 0.0 copy-done.6
  42.5 8.6 %render.1 = (f32[16,768]{1,0:T(8,128)}, f32[16,128]{1,0:T(8,128)S(1)}, f32[384,128]{1,0:T(8,128)}) custom-call(bf16[1536,128]{1,0:T(8,128)(2,1)S(1)} %bitcast.8, s32[16,128]{1,0:T(8,128)S(1)} %copy-done.3, s32[16,128]{1,0:T(8,128)S(1)} %copy-done.4, s32[16]{0:T(128)S(1)} %copy-done.6, s32[16]{0:T(128)S(1)} %copy-done.5), custom_call_target="tpu_custom_call" | custom-call | tf_op jit(solution)/shard_map/render/pallas_call | solution.py:728
  51.1 4.6 %all-to-all-start.2 = ((f32[128,1,384]{2,1,0:T(1,128)}), f32[128,1,384]{2,1,0:T(1,128)S(1)}, u32[]{:S(2)}, u32[]{:S(2)}) async-start(f32[128,1,384]{2,1,0:T(1,128)} %bitcast.5), calls=%async_computation.2 | async-start | bytes 393216 | tf_op jit(solution)/shard_map/all_to_all | solution.py:683
  55.8 0.6 slice_reduce_fusion
  56.4 9.9 %all-to-all-done.2 = f32[128,1,384]{2,1,0:T(1,128)S(1)} async-done(((f32[128,1,384]{2,1,0:T(1,128)}), f32[128,1,384]{2,1,0:T(1,128)S(1)}, u32[]{:S(2)}, u32[]{:S(2)}) %all-to-all-start.2) | async-done | bytes 196640 | tf_op jit(solution)/shard_map/all_to_all | solution.py:683
  66.3 0.0 copy-done.1
  66.3 3.7 %update.1 = f32[59,8192]{1,0:T(8,128)} custom-call(f32[384,128]{1,0:T(8,128)S(1)} %bitcast.10, s32[128,128]{1,0:T(8,128)S(1)} %bitcast.12, f32[59,8192]{1,0:T(8,128)S(1)} %copy-done.1), custom_call_target="tpu_custom_call" | custom-call | tf_op jit(solution)/shard_map/update/pallas_call | solution.py:753
Async XLA Ops:
  0.6 23.3 %copy-start.2 = (bf16[16,768]{1,0:T(8,128)(2,1)S(1)}, bf16[16,768]{1,0:T(8,128)(2,1)}, u32[]{:S(2)}) copy-start(bf16[16,768]{1,0:T(8,128)(2,1)} %image_ref.1) | copy-start | bytes 73732
  3.1 20.8 %all-to-all-start = ((s32[128,1,128]{2,1,0:T(1,128)}), s32[128,1,128]{2,1,0:T(1,128)S(1)}, u32[]{:S(2)}, u32[]{:S(2)}) async-start(s32[128,1,128]{2,1,0:T(1,128)} %bitcast.13), calls=%async_computation | async-start | bytes 131072 | tf_op jit(solution)/shard_map/all_to_all | solution.py:683
  14.6 1.6 %copy-start = (f32[59,8192]{1,0:T(8,128)S(1)}, f32[59,8192]{1,0:T(8,128)}, u32[]{:S(2)}) copy-start(f32[59,8192]{1,0:T(8,128)} %params_ref.3) | copy-start | bytes 5799940
  16.2 26.3 %copy-start.3 = (s32[16,128]{1,0:T(8,128)S(1)}, s32[16,128]{1,0:T(8,128)}, u32[]{:S(2)}) copy-start(s32[16,128]{1,0:T(8,128)} %get-tuple-element.10.holder_ref) | copy-start | bytes 24580
  16.2 26.3 %copy-start.4 = (s32[16,128]{1,0:T(8,128)S(1)}, s32[16,128]{1,0:T(8,128)}, u32[]{:S(2)}) copy-start(s32[16,128]{1,0:T(8,128)} %get-tuple-element.11.place_ref) | copy-start | bytes 24580
  16.2 26.3 %copy-start.5 = (s32[16]{0:T(128)S(1)}, s32[16]{0:T(128)}, u32[]{:S(2)}) copy-start(s32[16]{0:T(128)} %prev_ref.1) | copy-start | bytes 196
  16.2 26.3 %copy-start.6 = (s32[16]{0:T(128)S(1)}, s32[16]{0:T(128)}, u32[]{:S(2)}) copy-start(s32[16]{0:T(128)} %tile_ref.1) | copy-start | bytes 196
  16.2 50.1 %copy-start.1 = (f32[59,8192]{1,0:T(8,128)S(1)}, f32[59,8192]{1,0:T(8,128)}, u32[]{:S(2)}) copy-start(f32[59,8192]{1,0:T(8,128)} %params_ref.3) | copy-start | bytes 5799940
  51.1 15.1 %all-to-all-start.2 = ((f32[128,1,384]{2,1,0:T(1,128)}), f32[128,1,384]{2,1,0:T(1,128)S(1)}, u32[]{:S(2)}, u32[]{:S(2)}) async-start(f32[128,1,384]{2,1,0:T(1,128)} %bitcast.5), calls=%async_computation.2 | async-start | bytes 393216 | tf_op jit(solution)/shard_map/all_to_all | solution.py:683
